TPU v7x, 32 devices: a whole 2x2x4 slice. The times are simulated.
32 devices in a mesh: dp: 8 (over z, x), tensor: 4 (over y, core).
Axes of the slice: x: 2, y: 2, z: 4, core: 2. Of those that a mesh axis runs over, the one named last changes fastest.
Arguments:
- target: bfloat16 [16384, 768], P('dp'), may hold values from -6 to 6
- memory: bfloat16 [16384, 768], P('dp'), may hold values from -6 to 6
- cotangent: bfloat16 [16384, 768], P('dp'), may hold values from -6 to 6
- tgt_seg: int32 [16, 1024], P('dp'), may hold values from 0 to 3, never falling along the last dimension, each value on 1 to 512 neighbouring positions
- mem_seg: int32 [16, 1024], P('dp'), may hold values from 0 to 3, never falling along the last dimension, each value on 1 to 512 neighbouring positions
- pad_len: int32 [16], P('dp'), may hold values from 0 to 128
- step_count: int32 [], replicated, may hold values from 2 to 20
- self_in: float32 [3, 768, 768], P(None, 'dp', 'tensor'), may hold values from -0.21875 to 0.21875
- self_in_first: float32 [3, 768, 768], P(None, 'dp', 'tensor'), may hold values from -0.00021362305 to 0.00021362305
- self_in_second: float32 [3, 768, 768], P(None, 'dp', 'tensor'), may hold values from 1.059121e-10 to 4.236484e-10
- self_out: float32 [768, 768], P('tensor', 'dp'), may hold values from -1.75 to 1.75
- self_out_first: float32 [768, 768], P('tensor', 'dp'), may hold values from -5.340576e-05 to 5.340576e-05
- self_out_second: float32 [768, 768], P('tensor', 'dp'), may hold values from 6.619506e-12 to 2.6478025e-11
- cross_in: float32 [3, 768, 768], P(None, 'dp', 'tensor'), may hold values from -0.21875 to 0.21875
- cross_in_first: float32 [3, 768, 768], P(None, 'dp', 'tensor'), may hold values from -0.00021362305 to 0.00021362305
- cross_in_second: float32 [3, 768, 768], P(None, 'dp', 'tensor'), may hold values from 1.059121e-10 to 4.236484e-10
- cross_out: float32 [768, 768], P('tensor', 'dp'), may hold values from -1.75 to 1.75
- cross_out_first: float32 [768, 768], P('tensor', 'dp'), may hold values from -2.2888184e-05 to 2.2888184e-05
- cross_out_second: float32 [768, 768], P('tensor', 'dp'), may hold values from 1.059121e-12 to 4.236484e-12
- ffn_in: float32 [768, 3072], P('dp', 'tensor'), may hold values from -0.21875 to 0.21875
- ffn_in_first: float32 [768, 3072], P('dp', 'tensor'), may hold values from -0.00021362305 to 0.00021362305
- ffn_in_second: float32 [768, 3072], P('dp', 'tensor'), may hold values from 1.059121e-10 to 4.236484e-10
- ffn_out: float32 [3072, 768], P('tensor', 'dp'), may hold values from -0.28867513 to 0.28867513
- ffn_out_first: float32 [3072, 768], P('tensor', 'dp'), may hold values from -0.00021362305 to 0.00021362305
- ffn_out_second: float32 [3072, 768], P('tensor', 'dp'), may hold values from 1.059121e-10 to 4.236484e-10
- norm_params: float32 [6, 768], P(None, 'dp'), may hold values from -0.8 to 3.6, as said below
- norm_params_first: float32 [6, 768], P(None, 'dp'), may hold values from -0.00061035156 to 0.00061035156
- norm_params_second: float32 [6, 768], P(None, 'dp'), may hold values from 9.532088e-10 to 3.8128354e-09
Outputs:
- global_norm: float32 [], replicated
- block_out: float32 [16384, 768], P('dp')
- grad_target: float32 [16384, 768], P('dp')
- grad_memory: float32 [16384, 768], P('dp')
- self_in_new: float32 [3, 768, 768], P(None, 'dp', 'tensor')
- self_in_copy: bfloat16 [3, 768, 768], P(None, 'dp', 'tensor')
- self_in_first_new: float32 [3, 768, 768], P(None, 'dp', 'tensor')
- self_in_second_new: float32 [3, 768, 768], P(None, 'dp', 'tensor')
- self_out_new: float32 [768, 768], P('tensor', 'dp')
- self_out_copy: bfloat16 [768, 768], P('tensor', 'dp')
- self_out_first_new: float32 [768, 768], P('tensor', 'dp')
- self_out_second_new: float32 [768, 768], P('tensor', 'dp')
- cross_in_new: float32 [3, 768, 768], P(None, 'dp', 'tensor')
- cross_in_copy: bfloat16 [3, 768, 768], P(None, 'dp', 'tensor')
- cross_in_first_new: float32 [3, 768, 768], P(None, 'dp', 'tensor')
- cross_in_second_new: float32 [3, 768, 768], P(None, 'dp', 'tensor')
- cross_out_new: float32 [768, 768], P('tensor', 'dp')
- cross_out_copy: bfloat16 [768, 768], P('tensor', 'dp')
- cross_out_first_new: float32 [768, 768], P('tensor', 'dp')
- cross_out_second_new: float32 [768, 768], P('tensor', 'dp')
- ffn_in_new: float32 [768, 3072], P('dp', 'tensor')
- ffn_in_copy: bfloat16 [768, 3072], P('dp', 'tensor')
- ffn_in_first_new: float32 [768, 3072], P('dp', 'tensor')
- ffn_in_second_new: float32 [768, 3072], P('dp', 'tensor')
- ffn_out_new: float32 [3072, 768], P('tensor', 'dp')
- ffn_out_copy: bfloat16 [3072, 768], P('tensor', 'dp')
- ffn_out_first_new: float32 [3072, 768], P('tensor', 'dp')
- ffn_out_second_new: float32 [3072, 768], P('tensor', 'dp')
- norm_params_new: float32 [6, 768], P(None, 'dp')
- norm_params_copy: bfloat16 [6, 768], P(None, 'dp')
- norm_params_first_new: float32 [6, 768], P(None, 'dp')
- norm_params_second_new: float32 [6, 768], P(None, 'dp')
Inputs may be any that keep to these rules, and one draw needn't show every extreme that they name: `tgt_seg`: in each row the ids never fall and each of the 4 ids occurs. `mem_seg`: in each row the ids never fall and each of the 4 ids occurs. `norm_params`: rows 0 to 2 are positive gains, rows 3 to 5 shifts.
All inputs are finite; a program needn't handle non-finite values.
Results may differ from a plain program's by a relative error of at most 0.039.
Values may be sent and summed in bfloat16 or wider, within the bound.
A program may use at most 192 MiB of HBM per device.

v0:
```python
from functools import partial
import math

import jax
import jax.numpy as jnp
from jax import lax
from jax.sharding import PartitionSpec as P

HD = 64


EPS_NORM = 1e-05
NEG_FILL = -1000000000.0
BETA_ONE = 0.9
BETA_TWO = 0.999
EPS_ADAM = 1e-08
RATE_MATRIX = 0.05
RATE_OUTPUT = 0.25
RATE_NORMS = 0.75
DECAY_RATE = 0.1
CLIP_LIMIT = 1.0
GELU_COEF = 0.044715


def gelu_with_slope(values):
    root_coef = math.sqrt(2.0 / math.pi)
    inner = root_coef * (values + GELU_COEF * values * values * values)
    tangent = jnp.tanh(inner)
    output = 0.5 * values * (1.0 + tangent)
    slope = 0.5 * (1.0 + tangent) + 0.5 * values * (1.0 - tangent * tangent) * root_coef * (
        1.0 + 3.0 * GELU_COEF * values * values
    )
    return (output, slope)


def norm_forward(values, norm_gain, norm_shift):
    centre = values - jnp.mean(values, -1, keepdims=True)
    inverse = lax.rsqrt(jnp.mean(centre * centre, -1, keepdims=True) + EPS_NORM)
    scaled = centre * inverse
    return (scaled, inverse, (scaled * norm_gain + norm_shift).astype(jnp.bfloat16))


def norm_backward(upstream, scaled, inverse, norm_gain):
    weighted = upstream * norm_gain
    result = inverse * (
        weighted
        - jnp.mean(weighted, -1, keepdims=True)
        - scaled * jnp.mean(weighted * scaled, -1, keepdims=True)
    )
    return (result, jnp.sum(upstream * scaled, 0), jnp.sum(upstream, 0))


def self_mask(tgt_ids, valid_len, offset, row_span):
    query_pos = offset + jnp.arange(row_span, dtype=jnp.int32)
    key_pos = jnp.arange(tgt_ids.shape[0], dtype=jnp.int32)
    query_ids = lax.dynamic_slice_in_dim(tgt_ids, offset, row_span)
    causal = key_pos[None, :] <= query_pos[:, None]
    same_doc = query_ids[:, None] == tgt_ids[None, :]
    live_key = (key_pos[None, :] < valid_len) | (key_pos[None, :] == query_pos[:, None])
    return causal & same_doc & live_key


def cross_mask(tgt_ids, mem_ids, offset, row_span):
    query_ids = lax.dynamic_slice_in_dim(tgt_ids, offset, row_span)
    return query_ids[:, None] == mem_ids[None, :]


def block_scores(query_block, key_heads, mask_fn, offset, block_rows):
    scores = jnp.einsum(
        "qhd,khd->hqk", query_block, key_heads, preferred_element_type=jnp.float32
    ) * (1.0 / math.sqrt(HD))
    return jnp.where(mask_fn(offset, block_rows)[None], scores, NEG_FILL)


def attend_rows(query_rows, key_rows, value_rows, mask_fn):
    row_length, col_width = query_rows.shape
    head_count = col_width // HD
    block_rows = min(512, row_length)
    key_heads = key_rows.reshape(-1, head_count, HD)
    value_heads = value_rows.reshape(-1, head_count, HD)

    def one_block(offset):
        query_block = lax.dynamic_slice_in_dim(query_rows, offset, block_rows).reshape(
            block_rows, head_count, HD
        )
        scores = block_scores(query_block, key_heads, mask_fn, offset, block_rows)
        row_peak = jnp.max(scores, -1, keepdims=True)
        shifted = jnp.exp(scores - row_peak)
        totals = jnp.sum(shifted, -1, keepdims=True)
        attn_weights = (shifted / totals).astype(jnp.bfloat16)
        attended = jnp.einsum(
            "hqk,khd->qhd", attn_weights, value_heads, preferred_element_type=jnp.float32
        )
        return (attended.reshape(block_rows, col_width), row_peak + jnp.log(totals))

    offsets = jnp.arange(row_length // block_rows, dtype=jnp.int32) * block_rows
    attended, logsum = lax.map(one_block, offsets)
    return (attended.reshape(row_length, col_width), logsum)


def attend_back(query_rows, key_rows, value_rows, grad_rows, logsum, mask_fn):
    row_length, col_width = query_rows.shape
    head_count = col_width // HD
    block_rows = min(512, row_length)
    score_scale = 1.0 / math.sqrt(HD)
    key_heads = key_rows.reshape(-1, head_count, HD)
    value_heads = value_rows.reshape(-1, head_count, HD)

    def one_block(running, packed):
        offset, block_logsum = packed
        key_grad, value_grad = running
        query_block = lax.dynamic_slice_in_dim(query_rows, offset, block_rows).reshape(
            block_rows, head_count, HD
        )
        grad_block = lax.dynamic_slice_in_dim(grad_rows, offset, block_rows).reshape(
            block_rows, head_count, HD
        )
        scores = block_scores(query_block, key_heads, mask_fn, offset, block_rows)
        attn_weights = jnp.exp(scores - block_logsum)
        weight_grad = jnp.einsum(
            "qhd,khd->hqk", grad_block, value_heads, preferred_element_type=jnp.float32
        )
        inner_sum = jnp.sum(attn_weights * weight_grad, -1, keepdims=True)
        score_grad = (attn_weights * (weight_grad - inner_sum)).astype(jnp.bfloat16)
        query_grad = (
            jnp.einsum("hqk,khd->qhd", score_grad, key_heads, preferred_element_type=jnp.float32)
            * score_scale
        )
        key_grad = (
            key_grad
            + jnp.einsum(
                "hqk,qhd->khd", score_grad, query_block, preferred_element_type=jnp.float32
            )
            * score_scale
        )
        value_grad = value_grad + jnp.einsum(
            "hqk,qhd->khd",
            attn_weights.astype(jnp.bfloat16),
            grad_block,
            preferred_element_type=jnp.float32,
        )
        return ((key_grad, value_grad), query_grad.reshape(block_rows, col_width))

    offsets = jnp.arange(row_length // block_rows, dtype=jnp.int32) * block_rows
    empty_grad = jnp.zeros((key_rows.shape[0], head_count, HD), jnp.float32)
    finals, query_grad = lax.scan(one_block, (empty_grad, empty_grad), (offsets, logsum))
    return (
        query_grad.reshape(row_length, col_width),
        finals[0].reshape(-1, col_width),
        finals[1].reshape(-1, col_width),
    )


def adam_update(weight, gradient, first, second, clip_factor, step_float, rate, decay):
    scaled = gradient * clip_factor
    first_new = BETA_ONE * first + (1.0 - BETA_ONE) * scaled
    second_new = BETA_TWO * second + (1.0 - BETA_TWO) * scaled * scaled
    first_hat = first_new / (1.0 - jnp.power(BETA_ONE, step_float))
    second_hat = second_new / (1.0 - jnp.power(BETA_TWO, step_float))
    weight_new = weight - rate * (first_hat / (jnp.sqrt(second_hat) + EPS_ADAM) + decay * weight)
    return (weight_new, weight_new.astype(jnp.bfloat16), first_new, second_new)


def body(
    target,
    memory,
    cotangent,
    tgt_seg,
    mem_seg,
    pad_len,
    step_count,
    self_in,
    self_in_first,
    self_in_second,
    self_out,
    self_out_first,
    self_out_second,
    cross_in,
    cross_in_first,
    cross_in_second,
    cross_out,
    cross_out_first,
    cross_out_second,
    ffn_in,
    ffn_in_first,
    ffn_in_second,
    ffn_out,
    ffn_out_first,
    ffn_out_second,
    norm_params,
    norm_params_first,
    norm_params_second,
):
    masters = (self_in, self_out, cross_in, cross_out, ffn_in, ffn_out, norm_params)
    halves = tuple((weight.astype(jnp.bfloat16) for weight in masters))
    proj_self_in, proj_self_out, proj_cross_in, proj_cross_out, proj_up, proj_down, norm_copy = (
        lax.all_gather(halves[0], "dp", axis=1, tiled=True),
        lax.all_gather(halves[1], "dp", axis=1, tiled=True),
        lax.all_gather(halves[2], "dp", axis=1, tiled=True),
        lax.all_gather(halves[3], "dp", axis=1, tiled=True),
        lax.all_gather(halves[4], "dp", axis=0, tiled=True),
        lax.all_gather(halves[5], "dp", axis=1, tiled=True),
        lax.all_gather(halves[6], "dp", axis=1, tiled=True),
    )
    gains = norm_copy.astype(jnp.float32)
    row_count, tgt_length = tgt_seg.shape
    mem_length = mem_seg.shape[1]
    tok_count = row_count * tgt_length
    col_width = proj_self_in.shape[2]
    valid_lens = tgt_length - pad_len
    inputs_float = target.astype(jnp.float32)
    scaled_one, inverse_one, normed_one = norm_forward(inputs_float, gains[0], gains[3])
    self_qkv = jnp.einsum(
        "td,sdc->stc", normed_one, proj_self_in, preferred_element_type=jnp.float32
    ).astype(jnp.bfloat16)
    self_rows = self_qkv.reshape(3, row_count, tgt_length, col_width)

    def self_forward(packed):
        query_row, key_row, value_row, tgt_row, valid_len = packed
        return attend_rows(query_row, key_row, value_row, partial(self_mask, tgt_row, valid_len))

    self_att, self_logsum = lax.map(
        self_forward, (self_rows[0], self_rows[1], self_rows[2], tgt_seg, valid_lens)
    )
    self_att = self_att.reshape(tok_count, col_width).astype(jnp.bfloat16)
    hidden_one = inputs_float + lax.psum(
        jnp.dot(self_att, proj_self_out, preferred_element_type=jnp.float32).astype(jnp.bfloat16),
        "tensor",
    ).astype(jnp.float32)
    scaled_two, inverse_two, normed_two = norm_forward(hidden_one, gains[1], gains[4])
    cross_query = jnp.dot(normed_two, proj_cross_in[0], preferred_element_type=jnp.float32).astype(
        jnp.bfloat16
    )
    cross_kv = jnp.einsum(
        "md,sdc->smc", memory, proj_cross_in[1:], preferred_element_type=jnp.float32
    ).astype(jnp.bfloat16)
    query_rows = cross_query.reshape(row_count, tgt_length, col_width)
    kv_rows = cross_kv.reshape(2, row_count, mem_length, col_width)

    def cross_forward(packed):
        query_row, key_row, value_row, tgt_row, mem_row = packed
        return attend_rows(query_row, key_row, value_row, partial(cross_mask, tgt_row, mem_row))

    cross_att, cross_logsum = lax.map(
        cross_forward, (query_rows, kv_rows[0], kv_rows[1], tgt_seg, mem_seg)
    )
    cross_att = cross_att.reshape(tok_count, col_width).astype(jnp.bfloat16)
    hidden_two = hidden_one + lax.psum(
        jnp.dot(cross_att, proj_cross_out, preferred_element_type=jnp.float32).astype(jnp.bfloat16),
        "tensor",
    ).astype(jnp.float32)
    scaled_three, inverse_three, normed_three = norm_forward(hidden_two, gains[2], gains[5])
    pre_act = jnp.dot(normed_three, proj_up, preferred_element_type=jnp.float32)
    activated, act_slope = gelu_with_slope(pre_act)
    hidden_ffn = activated.astype(jnp.bfloat16)
    block_out = hidden_two + lax.psum(
        jnp.dot(hidden_ffn, proj_down, preferred_element_type=jnp.float32).astype(jnp.bfloat16),
        "tensor",
    ).astype(jnp.float32)
    residual_grad = cotangent.astype(jnp.float32)
    out_grad = residual_grad.astype(jnp.bfloat16)
    grad_down = jnp.einsum("tf,td->fd", hidden_ffn, out_grad, preferred_element_type=jnp.float32)
    hidden_grad = jnp.einsum("td,fd->tf", out_grad, proj_down, preferred_element_type=jnp.float32)
    pre_grad = (hidden_grad * act_slope).astype(jnp.bfloat16)
    grad_up = jnp.einsum("td,tf->df", normed_three, pre_grad, preferred_element_type=jnp.float32)
    normed_grad = lax.psum(
        jnp.einsum("tf,df->td", pre_grad, proj_up, preferred_element_type=jnp.float32).astype(
            jnp.bfloat16
        ),
        "tensor",
    ).astype(jnp.float32)
    delta_three, gain_three, shift_three = norm_backward(
        normed_grad, scaled_three, inverse_three, gains[2]
    )
    residual_grad = residual_grad + delta_three
    out_grad = residual_grad.astype(jnp.bfloat16)
    grad_cross_out = jnp.einsum(
        "tc,td->cd", cross_att, out_grad, preferred_element_type=jnp.float32
    )
    att_grad = jnp.einsum(
        "td,cd->tc", out_grad, proj_cross_out, preferred_element_type=jnp.float32
    ).astype(jnp.bfloat16)

    def cross_backward(packed):
        query_row, key_row, value_row, grad_row, logsum_row, tgt_row, mem_row = packed
        return attend_back(
            query_row,
            key_row,
            value_row,
            grad_row,
            logsum_row,
            partial(cross_mask, tgt_row, mem_row),
        )

    query_grad, key_grad, value_grad = lax.map(
        cross_backward,
        (
            query_rows,
            kv_rows[0],
            kv_rows[1],
            att_grad.reshape(row_count, tgt_length, col_width),
            cross_logsum,
            tgt_seg,
            mem_seg,
        ),
    )
    query_low = query_grad.reshape(tok_count, col_width).astype(jnp.bfloat16)
    kv_low = (
        jnp.stack([key_grad, value_grad])
        .reshape(2, row_count * mem_length, col_width)
        .astype(jnp.bfloat16)
    )
    grad_cross_in = jnp.concatenate(
        [
            jnp.einsum("td,tc->dc", normed_two, query_low, preferred_element_type=jnp.float32)[
                None
            ],
            jnp.einsum("md,smc->sdc", memory, kv_low, preferred_element_type=jnp.float32),
        ],
        0,
    )
    query_part = jnp.einsum(
        "tc,dc->td", query_low, proj_cross_in[0], preferred_element_type=jnp.float32
    )
    memory_part = jnp.einsum(
        "smc,sdc->md", kv_low, proj_cross_in[1:], preferred_element_type=jnp.float32
    )
    normed_grad, memory_grad = (
        lax.psum(query_part.astype(jnp.bfloat16), "tensor").astype(jnp.float32),
        lax.psum(memory_part.astype(jnp.bfloat16), "tensor").astype(jnp.float32),
    )
    delta_two, gain_two, shift_two = norm_backward(normed_grad, scaled_two, inverse_two, gains[1])
    residual_grad = residual_grad + delta_two
    out_grad = residual_grad.astype(jnp.bfloat16)
    grad_self_out = jnp.einsum("tc,td->cd", self_att, out_grad, preferred_element_type=jnp.float32)
    att_grad = jnp.einsum(
        "td,cd->tc", out_grad, proj_self_out, preferred_element_type=jnp.float32
    ).astype(jnp.bfloat16)

    def self_backward(packed):
        query_row, key_row, value_row, grad_row, logsum_row, tgt_row, valid_len = packed
        return attend_back(
            query_row,
            key_row,
            value_row,
            grad_row,
            logsum_row,
            partial(self_mask, tgt_row, valid_len),
        )

    query_grad, key_grad, value_grad = lax.map(
        self_backward,
        (
            self_rows[0],
            self_rows[1],
            self_rows[2],
            att_grad.reshape(row_count, tgt_length, col_width),
            self_logsum,
            tgt_seg,
            valid_lens,
        ),
    )
    qkv_low = (
        jnp.stack([query_grad, key_grad, value_grad])
        .reshape(3, tok_count, col_width)
        .astype(jnp.bfloat16)
    )
    grad_self_in = jnp.einsum(
        "td,stc->sdc", normed_one, qkv_low, preferred_element_type=jnp.float32
    )
    normed_grad = lax.psum(
        jnp.einsum("stc,sdc->td", qkv_low, proj_self_in, preferred_element_type=jnp.float32).astype(
            jnp.bfloat16
        ),
        "tensor",
    ).astype(jnp.float32)
    delta_one, gain_one, shift_one = norm_backward(normed_grad, scaled_one, inverse_one, gains[0])
    grad_target = residual_grad + delta_one
    grad_norms = jnp.stack([gain_one, gain_two, gain_three, shift_one, shift_two, shift_three])
    (
        reduced_self_in,
        reduced_self_out,
        reduced_cross_in,
        reduced_cross_out,
        reduced_up,
        reduced_down,
        reduced_norms,
    ) = (
        lax.psum_scatter(grad_self_in, "dp", scatter_dimension=1, tiled=True),
        lax.psum_scatter(grad_self_out, "dp", scatter_dimension=1, tiled=True),
        lax.psum_scatter(grad_cross_in, "dp", scatter_dimension=1, tiled=True),
        lax.psum_scatter(grad_cross_out, "dp", scatter_dimension=1, tiled=True),
        lax.psum_scatter(grad_up, "dp", scatter_dimension=0, tiled=True),
        lax.psum_scatter(grad_down, "dp", scatter_dimension=1, tiled=True),
        lax.psum_scatter(grad_norms, "dp", scatter_dimension=1, tiled=True),
    )
    local_squares = jnp.sum(reduced_norms * reduced_norms) / lax.axis_size("tensor")
    for reduced in (
        reduced_self_in,
        reduced_self_out,
        reduced_cross_in,
        reduced_cross_out,
        reduced_up,
        reduced_down,
    ):
        local_squares = local_squares + jnp.sum(reduced * reduced)
    global_norm = jnp.sqrt(lax.psum(local_squares, ("dp", "tensor")))
    clip_factor = CLIP_LIMIT / jnp.maximum(global_norm, CLIP_LIMIT)
    step_float = step_count.astype(jnp.float32)
    sin_new, sin_copy, sin_first, sin_second = adam_update(
        self_in,
        reduced_self_in,
        self_in_first,
        self_in_second,
        clip_factor,
        step_float,
        RATE_MATRIX,
        DECAY_RATE,
    )
    sout_new, sout_copy, sout_first, sout_second = adam_update(
        self_out,
        reduced_self_out,
        self_out_first,
        self_out_second,
        clip_factor,
        step_float,
        RATE_OUTPUT,
        DECAY_RATE,
    )
    cin_new, cin_copy, cin_first, cin_second = adam_update(
        cross_in,
        reduced_cross_in,
        cross_in_first,
        cross_in_second,
        clip_factor,
        step_float,
        RATE_MATRIX,
        DECAY_RATE,
    )
    cout_new, cout_copy, cout_first, cout_second = adam_update(
        cross_out,
        reduced_cross_out,
        cross_out_first,
        cross_out_second,
        clip_factor,
        step_float,
        RATE_OUTPUT,
        DECAY_RATE,
    )
    fin_new, fin_copy, fin_first, fin_second = adam_update(
        ffn_in,
        reduced_up,
        ffn_in_first,
        ffn_in_second,
        clip_factor,
        step_float,
        RATE_MATRIX,
        DECAY_RATE,
    )
    fout_new, fout_copy, fout_first, fout_second = adam_update(
        ffn_out,
        reduced_down,
        ffn_out_first,
        ffn_out_second,
        clip_factor,
        step_float,
        RATE_MATRIX,
        DECAY_RATE,
    )
    norm_new, norm_half, norm_first, norm_second = adam_update(
        norm_params,
        reduced_norms,
        norm_params_first,
        norm_params_second,
        clip_factor,
        step_float,
        RATE_NORMS,
        0.0,
    )
    return (
        global_norm,
        block_out,
        grad_target,
        memory_grad,
        sin_new,
        sin_copy,
        sin_first,
        sin_second,
        sout_new,
        sout_copy,
        sout_first,
        sout_second,
        cin_new,
        cin_copy,
        cin_first,
        cin_second,
        cout_new,
        cout_copy,
        cout_first,
        cout_second,
        fin_new,
        fin_copy,
        fin_first,
        fin_second,
        fout_new,
        fout_copy,
        fout_first,
        fout_second,
        norm_new,
        norm_half,
        norm_first,
        norm_second,
    )


def solution(mesh):
    return jax.shard_map(
        body,
        mesh=mesh,
        in_specs=(
            P("dp", None),
            P("dp", None),
            P("dp", None),
            P("dp", None),
            P("dp", None),
            P("dp"),
            P(),
            P(None, "dp", "tensor"),
            P(None, "dp", "tensor"),
            P(None, "dp", "tensor"),
            P("tensor", "dp"),
            P("tensor", "dp"),
            P("tensor", "dp"),
            P(None, "dp", "tensor"),
            P(None, "dp", "tensor"),
            P(None, "dp", "tensor"),
            P("tensor", "dp"),
            P("tensor", "dp"),
            P("tensor", "dp"),
            P("dp", "tensor"),
            P("dp", "tensor"),
            P("dp", "tensor"),
            P("tensor", "dp"),
            P("tensor", "dp"),
            P("tensor", "dp"),
            P(None, "dp"),
            P(None, "dp"),
            P(None, "dp"),
        ),
        out_specs=(
            P(),
            P("dp", None),
            P("dp", None),
            P("dp", None),
            P(None, "dp", "tensor"),
            P(None, "dp", "tensor"),
            P(None, "dp", "tensor"),
            P(None, "dp", "tensor"),
            P("tensor", "dp"),
            P("tensor", "dp"),
            P("tensor", "dp"),
            P("tensor", "dp"),
            P(None, "dp", "tensor"),
            P(None, "dp", "tensor"),
            P(None, "dp", "tensor"),
            P(None, "dp", "tensor"),
            P("tensor", "dp"),
            P("tensor", "dp"),
            P("tensor", "dp"),
            P("tensor", "dp"),
            P("dp", "tensor"),
            P("dp", "tensor"),
            P("dp", "tensor"),
            P("dp", "tensor"),
            P("tensor", "dp"),
            P("tensor", "dp"),
            P("tensor", "dp"),
            P("tensor", "dp"),
            P(None, "dp"),
            P(None, "dp"),
            P(None, "dp"),
            P(None, "dp"),
        ),
        check_vma=False,
    )
```

profile of v0, /device:TPU:0, one launch (start us, length us, event | category | flops | bytes accessed | tf_op | source)
XLA Modules:
  0.0 1301.8 jit_solution(7784693598265582769)
XLA Ops:
  15.5 27.8 %all-gather = bf16[8,96,6]{1,2,0:T(8,128)(2,1)S(1)} all-gather(bf16[1,96,6]{1,2,0:T(8,128)(2,1)S(1)} %convert_bitcast_fusion.1), channel_id=1, replica_groups=mesh['dp'=8,'tensor'=4] {'dp'}, dimensions={0}, use_global_device_ids=true | all-gather | bytes 10368 | tf_op jit(solution)/shard_map/all_gather | solution.py:203
  47.8 33.2 %all_gather.23 = bf16[192,768]{0,1:T(8,128)(2,1)} all-gather(bf16[192,96]{0,1:T(8,128)(2,1)} %copy.266), channel_id=1, replica_groups=mesh['dp'=8,'tensor'=4] {'dp'}, dimensions={1}, use_global_device_ids=true | all-gather | bytes 331776 | tf_op jit(solution)/shard_map/all_gather | solution.py:198
  81.1 37.2 %all_gather.22 = bf16[3,768,192]{2,0,1:T(4,128)(2,1)} all-gather(bf16[3,96,192]{2,0,1:T(4,128)(2,1)S(1)} %copy.261), channel_id=1, replica_groups=mesh['dp'=8,'tensor'=4] {'dp'}, dimensions={1}, use_global_device_ids=true | all-gather | bytes 995328 | tf_op jit(solution)/shard_map/all_gather | solution.py:197
  121.9 4.3 fusion.125
  146.2 71.5 %while.107 = (s32[]{:T(128)}, bf16[2,1024,192]{2,1,0:T(8,128)(2,1)}, f32[2,2,3,512,1]{3,2,1,4,0:T(4,128)}, bf16[2,1024,192]{1,2,0:T(8,128)(2,1)}, bf16[2,1024,19...) while((s32[]{:T(128)}, bf16[2,1024,192]{2,1,0:T(8,128)(2,1)}, ...), condition=%wide.region_7.8_spmd, body=%wide.region_2.7_spmd.sunk | while | flops 424673280 | bytes 32062052 | solution.py:222
  151.1 25.5 %while.114 = (s32[]{:T(128)}, bf16[2,512,192]{1,2,0:T(8,128)(2,1)}, f32[2,3,512,1]{2,1,3,0:T(4,128)}, s32[2]{0:T(128)S(1)}, s32[1024]{0:T(1024)S(1)}, /*index=5*...) while((s32[]{:T(128)}, bf16[2,512,192]{1,2,0:T(8,128)(2,1)}, ...), condition=%wide.region_6.6_spmd, body=%wide.region_3.5_spmd.sunk | while | flops 424673280 | bytes 27826512 | solution.py:97
  186.8 25.5 %while.114 = (s32[]{:T(128)}, bf16[2,512,192]{1,2,0:T(8,128)(2,1)}, f32[2,3,512,1]{2,1,3,0:T(4,128)}, s32[2]{0:T(128)S(1)}, s32[1024]{0:T(1024)S(1)}, /*index=5*...) while((s32[]{:T(128)}, bf16[2,512,192]{1,2,0:T(8,128)(2,1)}, ...), condition=%wide.region_6.6_spmd, body=%wide.region_3.5_spmd.sunk | while | flops 424673280 | bytes 27826512 | solution.py:97
  217.7 4.1 convolution_convert_fusion.4
  222.0 33.8 %all_gather.24 = bf16[3,768,192]{2,0,1:T(4,128)(2,1)S(1)} all-gather(bf16[3,96,192]{2,0,1:T(4,128)(2,1)S(1)} %copy.267), channel_id=1, replica_groups=mesh['dp'=8,'tensor'=4] {'dp'}, dimensions={1}, use_global_device_ids=true | all-gather | bytes 995328 | tf_op jit(solution)/shard_map/all_gather | solution.py:199
  279.9 33.0 %all_gather.25 = bf16[192,768]{0,1:T(8,128)(2,1)} all-gather(bf16[192,96]{0,1:T(8,128)(2,1)S(1)} %copy-done.58), channel_id=1, replica_groups=mesh['dp'=8,'tensor'=4] {'dp'}, dimensions={1}, use_global_device_ids=true | all-gather | bytes 331776 | tf_op jit(solution)/shard_map/all_gather | solution.py:200
  324.6 62.9 %while.109 = (s32[]{:T(128)}, bf16[2,1024,192]{2,1,0:T(8,128)(2,1)}, f32[2,2,3,512,1]{3,2,1,4,0:T(4,128)}, bf16[2,1024,192]{1,2,0:T(8,128)(2,1)}, bf16[2,1024,19...) while((s32[]{:T(128)}, bf16[2,1024,192]{2,1,0:T(8,128)(2,1)}, ...), condition=%wide.region_16.17_spmd, body=%wide.region_11.16_spmd.sunk | while | flops 422050304 | bytes 32064080 | solution.py:244
  329.0 21.8 %while.115 = (s32[]{:T(128)}, bf16[2,512,192]{1,2,0:T(8,128)(2,1)}, f32[2,3,512,1]{2,1,3,0:T(4,128)}, s32[2]{0:T(128)S(1)}, s32[1024]{0:T(1024)S(1)}, /*index=5*...) while((s32[]{:T(128)}, bf16[2,512,192]{1,2,0:T(8,128)(2,1)}, ...), condition=%wide.region_15.15_spmd, body=%wide.region_12.14_spmd.sunk | while | flops 422050304 | bytes 27820360 | solution.py:97
  360.5 21.8 %while.115 = (s32[]{:T(128)}, bf16[2,512,192]{1,2,0:T(8,128)(2,1)}, f32[2,3,512,1]{2,1,3,0:T(4,128)}, s32[2]{0:T(128)S(1)}, s32[1024]{0:T(1024)S(1)}, /*index=5*...) while((s32[]{:T(128)}, bf16[2,512,192]{1,2,0:T(8,128)(2,1)}, ...), condition=%wide.region_15.15_spmd, body=%wide.region_12.14_spmd.sunk | while | flops 422050304 | bytes 27820360 | solution.py:97
  394.1 67.0 %all-reduce.9.cloned.1.call-done = bf16[2048,768]{1,0:T(8,128)(2,1)} async-done(((bf16[2048,768]{1,0:T(8,128)(2,1)}), bf16[2048,768]{1,0:T(8,128)(2,1)}) %all-reduce.9.cloned.1.call-update) | async-done | bytes 3145744 | tf_op jit(solution)/shard_map/psum | solution.py:248
  461.1 5.2 fusion.142
  471.5 7.6 fusion.147
  479.7 7.9 fusion.78
  493.5 67.9 %all-reduce.11.cloned.1.call-done = bf16[2048,768]{1,0:T(8,128)(2,1)} async-done(((bf16[2048,768]{1,0:T(8,128)(2,1)}), bf16[2048,768]{1,0:T(8,128)(2,1)}) %all-reduce.11.cloned.1.call-update) | async-done | bytes 3145744 | tf_op jit(solution)/shard_map/psum | solution.py:266
  561.4 6.1 fusion.79
  567.5 4.9 fusion.70
  580.4 98.0 %while.111 = (s32[]{:T(128)}, bf16[2,1024,192]{2,1,0:T(8,128)(2,1)}, bf16[2,1024,192]{1,2,0:T(8,128)(2,1)}, bf16[2,1024,192]{1,2,0:T(8,128)(2,1)}, f32[2,2,3,512...) while((s32[]{:T(128)}, bf16[2,1024,192]{2,1,0:T(8,128)(2,1)}, ...), condition=%wide.region_27.28_spmd, body=%wide.region_23.27_spmd.sunk | while | flops 1031928320 | bytes 81294024 | solution.py:295
  586.9 34.5 %while.116 = (s32[]{:T(128)}, f32[1024,3,64]{0,2,1:T(8,128)}, f32[1024,3,64]{0,2,1:T(8,128)}, bf16[2,512,192]{1,2,0:T(8,128)(2,1)}, s32[2]{0:T(128)}, /*index=5*...) while((s32[]{:T(128)}, f32[1024,3,64]{0,2,1:T(8,128)}, ...), condition=%wide.region_26.26_spmd.clone, body=%wide.region_24.25_spmd.clone.sunk | while | flops 1031928320 | bytes 73126296 | solution.py:146
  635.8 34.5 %while.116 = (s32[]{:T(128)}, f32[1024,3,64]{0,2,1:T(8,128)}, f32[1024,3,64]{0,2,1:T(8,128)}, bf16[2,512,192]{1,2,0:T(8,128)(2,1)}, s32[2]{0:T(128)}, /*index=5*...) while((s32[]{:T(128)}, f32[1024,3,64]{0,2,1:T(8,128)}, ...), condition=%wide.region_26.26_spmd.clone, body=%wide.region_24.25_spmd.clone.sunk | while | flops 1031928320 | bytes 73126296 | solution.py:146
  682.4 5.3 fusion.107
  687.8 63.2 %all-reduce.13.cloned.1.call-done = bf16[2048,768]{1,0:T(8,128)(2,1)} async-done(((bf16[2048,768]{1,0:T(8,128)(2,1)}), bf16[2048,768]{1,0:T(8,128)(2,1)}) %all-reduce.13.cloned.1.call-update) | async-done | bytes 3145744 | tf_op jit(solution)/shard_map/psum | solution.py:329
  751.1 7.7 fusion.80
  758.8 5.2 fusion.66
  769.1 8.3 fusion.127
  777.5 6.9 fusion.148
  806.2 4.3 copy.315
  810.5 4.7 reshape.549
  823.3 100.3 %while.113 = (s32[]{:T(128)}, bf16[2,1024,192]{2,1,0:T(8,128)(2,1)}, bf16[2,1024,192]{1,2,0:T(8,128)(2,1)}, bf16[2,1024,192]{1,2,0:T(8,128)(2,1)}, f32[2,2,3,512...) while((s32[]{:T(128)}, bf16[2,1024,192]{2,1,0:T(8,128)(2,1)}, ...), condition=%wide.region_35.36_spmd, body=%wide.region_31.35_spmd.sunk | while | flops 1034551296 | bytes 81291992 | solution.py:351
  830.1 35.6 %while.117 = (s32[]{:T(128)}, f32[1024,3,64]{0,2,1:T(8,128)}, f32[1024,3,64]{0,2,1:T(8,128)}, bf16[2,512,192]{1,2,0:T(8,128)(2,1)}, s32[2]{0:T(128)S(1)}, /*inde...) while((s32[]{:T(128)}, f32[1024,3,64]{0,2,1:T(8,128)}, ...), condition=%wide.region_34.34_spmd.clone, body=%wide.region_32.33_spmd.clone.sunk | while | flops 1034551296 | bytes 73132440 | solution.py:146
  880.1 35.6 %while.117 = (s32[]{:T(128)}, f32[1024,3,64]{0,2,1:T(8,128)}, f32[1024,3,64]{0,2,1:T(8,128)}, bf16[2,512,192]{1,2,0:T(8,128)(2,1)}, s32[2]{0:T(128)S(1)}, /*inde...) while((s32[]{:T(128)}, f32[1024,3,64]{0,2,1:T(8,128)}, ...), condition=%wide.region_34.34_spmd.clone, body=%wide.region_32.33_spmd.clone.sunk | while | flops 1034551296 | bytes 73132440 | solution.py:146
  938.5 6.3 fusion.101
  944.8 4.2 copy.311
  949.0 4.7 reshape.545
  953.8 8.7 convolution_convert_fusion
  966.1 4.2 bitcast_convert_fusion.1
  992.3 52.0 %reduce-scatter.28.cloned.1.call-done = f32[96,576]{1,0:T(8,128)} async-done(((f32[768,576]{1,0:T(8,128)}), f32[96,576]{1,0:T(8,128)}) %reduce-scatter.28.cloned.1.call-update) | async-done | bytes 221200
  1048.0 66.5 %reduce-scatter.24.cloned.1.call-done = f32[96,576]{1,0:T(8,128)} async-done(((f32[768,576]{1,0:T(8,128)}), f32[96,576]{1,0:T(8,128)}) %reduce-scatter.24.cloned.1.call-update) | async-done | bytes 221200
  1119.9 21.2 %all-reduce.15.cloned.1.call-done = (bf16[2048,768]{1,0:T(8,128)(2,1)}, bf16[2048,768]{1,0:T(8,128)(2,1)}, bf16[2048,768]{1,0:T(8,128)(2,1)}) async-done(((bf16[2048,768]{1,0:T(8,128)(2,1)}, bf16[2048,768]{1,0:T(8,128)(2,1)}, bf16[2048,768]{1,0:T(8,128)(2,1)}), (bf16[2048,768]{1,0:T(8,128)(2,1)}, bf16[2048,768]{1,0:T(8,128)(2,1)}, bf16[2048,768]{1,0:T(8,128)(2,1)})) %all-reduce.15.cloned.1.call-update) | async-done | bytes 9437200 | tf_op jit(solution)/shard_map/psum | solution.py:371
  1141.2 5.0 fusion.63
  1151.7 7.6 fusion.61
  1159.2 6.1 convert_add_fusion.1
  1165.3 48.1 %reduce-scatter.22.cloned.1.call-done = f32[96,6]{1,0:T(8,128)} async-done(((f32[768,6]{1,0:T(8,128)}), f32[96,6]{1,0:T(8,128)}) %reduce-scatter.22.cloned.1.call-update) | async-done | bytes 2320
  1219.5 5.1 convert_element_type.221
  1224.6 40.1 %psum.61 = f32[]{:T(128)} all-reduce(f32[]{:T(128)S(6)} %add.355), channel_id=1, replica_groups=mesh['dp'=8,'tensor'=4] {'dp','tensor'}, use_global_device_ids=true, to_apply=%region_57.58 | all-reduce | flops 1 | bytes 8 | tf_op jit(solution)/shard_map/psum | solution.py:407
  (746 shorter events, 518.7 us)
Async XLA Ops:
  8.0 257.0 %copy-start = (bf16[2048,768]{1,0:T(8,128)(2,1)S(1)}, bf16[2048,768]{1,0:T(8,128)(2,1)}, u32[]{:S(2)}) copy-start(bf16[2048,768]{1,0:T(8,128)(2,1)} %param.45) | copy-start | bytes 9437188
  8.1 38.9 %copy-start.56 = (f32[192,96]{1,0:T(8,128)S(1)}, f32[192,96]{1,0:T(8,128)}, u32[]{:S(2)}) copy-start(f32[192,96]{1,0:T(8,128)} %param.54) | copy-start | bytes 221188
  8.1 39.6 %copy-start.41 = (f32[3,96,192]{2,1,0:T(8,128)S(1)}, f32[3,96,192]{2,1,0:T(8,128)}, u32[]{:S(2)}) copy-start(f32[3,96,192]{2,1,0:T(8,128)} %param.51) | copy-start | bytes 663556
  8.1 304.7 %all-reduce.7.cloned.1.call-start = ((), (), s32[]{:S(2)}) async-start(), calls=%async_computation.7 | async-start | bytes 6291456 | tf_op jit(solution)/shard_map/psum | solution.py:226
  12.5 113.7 %copy-start.59 = (f32[2048]{0:T(1024)}, f32[2048]{0:T(1024)S(1)}, u32[]{:S(2)}) copy-start(f32[2048]{0:T(1024)S(1)} %broadcast_multiply_fusion.8) | copy-start | bytes 24580
  15.5 110.7 %copy-start.63 = (f32[2048]{0:T(1024)}, f32[2048]{0:T(1024)S(1)}, u32[]{:S(2)}) copy-start(f32[2048]{0:T(1024)S(1)} %add_rsqrt_fusion.2) | copy-start | bytes 24580
  128.1 18.1 %copy-start.81 = (s32[2]{0:T(128)S(1)}, s32[2]{0:T(128)}, u32[]{:S(2)}) copy-start(s32[2]{0:T(128)} %broadcast_subtract_fusion) | copy-start | bytes 28
  217.7 41.2 %copy-start.57 = (f32[192,96]{1,0:T(8,128)S(1)}, f32[192,96]{1,0:T(8,128)}, u32[]{:S(2)}) copy-start(f32[192,96]{1,0:T(8,128)} %param.60) | copy-start | bytes 221188
  221.8 239.3 %all-reduce.9.cloned.1.call-start = ((), (), s32[]{:S(2)}) async-start(), calls=%async_computation.8 | async-start | bytes 6291456 | tf_op jit(solution)/shard_map/psum | solution.py:248
  261.9 57.7 %copy-start.40 = (bf16[1,768,192]{1,2,0:T(8,128)(2,1)}, bf16[1,768,192]{1,2,0:T(8,128)(2,1)S(1)}, u32[]{:S(2)}) copy-start(bf16[1,768,192]{1,2,0:T(8,128)(2,1)S(1)} %copy.319) | copy-start | bytes 884740
  267.5 12.4 copy-start.58
  391.6 79.9 %all-gather.6.cloned.1.call-start = ((), (), s32[]{:S(2)}) async-start(), calls=%async_computation.10 | async-start | bytes 1327104 | tf_op jit(solution)/shard_map/all_gather | solution.py:201
  392.4 87.4 %all-gather.4.cloned.1.call-start = ((), (), s32[]{:S(2)}) async-start(), calls=%async_computation.9 | async-start | bytes 1327104 | tf_op jit(solution)/shard_map/all_gather | solution.py:202
  394.1 167.3 %all-reduce.11.cloned.1.call-start = ((), (), s32[]{:S(2)}) async-start(), calls=%async_computation.11 | async-start | bytes 6291456 | tf_op jit(solution)/shard_map/psum | solution.py:266
  479.7 9.7 copy-start.80
  493.4 257.7 %all-reduce.13.cloned.1.call-start = ((), (), s32[]{:S(2)}) async-start(), calls=%async_computation.12 | async-start | bytes 6291456 | tf_op jit(solution)/shard_map/psum | solution.py:329
  567.5 7.7 copy-start.35
  682.3 68.7 %copy-start.62 = (f32[2048]{0:T(1024)S(1)}, f32[2048]{0:T(1024)}, u32[]{:S(2)}) copy-start(f32[2048]{0:T(1024)} %copy-done.61) | copy-start | bytes 24580
  682.3 68.7 %copy-start.66 = (f32[2048]{0:T(1024)S(1)}, f32[2048]{0:T(1024)}, u32[]{:S(2)}) copy-start(f32[2048]{0:T(1024)} %copy-done.65) | copy-start | bytes 24580
  682.3 68.7 %copy-start.69 = (f32[768]{0:T(1024)S(1)}, f32[768]{0:T(1024)}, u32[]{:S(2)}) copy-start(f32[768]{0:T(1024)} %get-tuple-element.913) | copy-start | bytes 9220
  682.4 300.9 %reduce-scatter.30.cloned.1.call-start = ((), (), s32[]{:S(2)}) async-start(), calls=%async_computation.19 | async-start | bytes 884736
  687.8 299.6 %reduce-scatter.26.cloned.1.call-start = ((), (), s32[]{:S(2)}) async-start(), calls=%async_computation.17 | async-start | bytes 884736
  751.1 7.7 copy-start.8
  751.1 7.7 copy-start.14
  751.1 7.7 copy-start.20
  758.8 8.0 copy-start.32
  769.1 219.9 %reduce-scatter.20.cloned.1.call-start = ((), (), s32[]{:S(2)}) async-start(), calls=%async_computation.14 | async-start | bytes 2654208 | tf_op jit(solution)/shard_map/reduce_scatter | solution.py:394
  777.4 213.3 %reduce-scatter.18.cloned.1.call-start = ((), (), s32[]{:S(2)}) async-start(), calls=%async_computation.13 | async-start | bytes 2654208 | tf_op jit(solution)/shard_map/reduce_scatter | solution.py:393
  784.4 259.9 %reduce-scatter.28.cloned.1.call-start = ((), (), s32[]{:S(2)}) async-start(), calls=%async_computation.18 | async-start | bytes 2211840
  806.2 9.0 copy-start.34
  815.2 8.1 copy-start.82
  815.2 299.3 %reduce-scatter.24.cloned.1.call-start = ((), (), s32[]{:S(2)}) async-start(), calls=%async_computation.16 | async-start | bytes 2211840
  923.6 14.9 %copy-start.60 = (f32[2048]{0:T(1024)S(1)}, f32[2048]{0:T(1024)}, u32[]{:S(2)}) copy-start(f32[2048]{0:T(1024)} %copy-done.59) | copy-start | bytes 24580
  923.6 14.9 %copy-start.64 = (f32[2048]{0:T(1024)S(1)}, f32[2048]{0:T(1024)}, u32[]{:S(2)}) copy-start(f32[2048]{0:T(1024)} %copy-done.63) | copy-start | bytes 24580
  923.6 14.9 %copy-start.70 = (f32[768]{0:T(1024)S(1)}, f32[768]{0:T(1024)}, u32[]{:S(2)}) copy-start(f32[768]{0:T(1024)} %get-tuple-element.915) | copy-start | bytes 9220
  923.6 14.9 %copy-start.77 = (f32[768]{0:T(1024)S(1)}, f32[768]{0:T(1024)}, u32[]{:S(2)}) copy-start(f32[768]{0:T(1024)} %get-tuple-element.914) | copy-start | bytes 9220
  953.7 187.5 %all-reduce.15.cloned.1.call-start = ((), (), s32[]{:S(2)}) async-start(), calls=%async_computation.20 | async-start | bytes 18874368 | tf_op jit(solution)/shard_map/psum | solution.py:371
  953.7 8.8 copy-start.49
  953.7 8.8 copy-start.55
  970.3 11.7 copy-start.72
  970.3 12.3 copy-start.71
  970.3 243.1 %reduce-scatter.22.cloned.1.call-start = ((), (), s32[]{:S(2)}) async-start(), calls=%async_computation.15 | async-start | bytes 442368
  988.4 57.8 %copy-start.45 = (f32[192,96]{1,0:T(8,128)}, f32[192,96]{1,0:T(8,128)S(1)}, u32[]{:S(2)}) copy-start(f32[192,96]{1,0:T(8,128)S(1)} %copy.314) | copy-start | bytes 221188
  1151.7 7.6 copy-start.37
  1224.6 59.8 %copy-start.74 = (f32[6,96]{1,0:T(8,128)S(1)}, f32[6,96]{1,0:T(8,128)}, u32[]{:S(2)}) copy-start(f32[6,96]{1,0:T(8,128)} %param.69) | copy-start | bytes 6916
  1224.6 59.8 %copy-start.75 = (f32[6,96]{1,0:T(8,128)S(1)}, f32[6,96]{1,0:T(8,128)}, u32[]{:S(2)}) copy-start(f32[6,96]{1,0:T(8,128)} %param.71) | copy-start | bytes 6916
  1224.6 59.8 %copy-start.76 = (f32[6,96]{1,0:T(8,128)S(1)}, f32[6,96]{1,0:T(8,128)}, u32[]{:S(2)}) copy-start(f32[6,96]{1,0:T(8,128)} %param.70) | copy-start | bytes 6916
  1271.6 19.2 %copy-start.39 = (f32[768,96]{0,1:T(8,128)S(1)}, f32[768,96]{0,1:T(8,128)}, u32[]{:S(2)}) copy-start(f32[768,96]{0,1:T(8,128)} %param.66) | copy-start | bytes 884740
  (122 other events, 304.3 us)
Sparse Core Ops, SparseCore 0:
  221.9 66.4 all-reduce.6
  391.7 69.3 all-reduce.8
  493.5 67.7 all-reduce.10
  682.5 68.5 all-reduce.12
  970.5 170.6 all-reduce.14
Sparse Core Ops, SparseCore 1:
  394.8 42.3 all-gather.5
  439.8 39.9 all-gather.3
  687.9 62.7 reduce-scatter.29
  769.2 62.7 reduce-scatter.25
  835.4 68.0 reduce-scatter.19
  907.0 68.0 reduce-scatter.17
  978.4 65.8 reduce-scatter.27
  1048.0 66.4 reduce-scatter.23
  1151.7 61.7 reduce-scatter.21
where the time goes:
time: 1310 us; the launch traced here: 1300 us
  waiting for transfers between devices  387 us (30%)
  local copies, waits for them, and re-layouts  319 us (24%)
  blocking collectives  205 us (16%)
  matrix products  183 us (14%)
  other arithmetic  150 us (11%)
  loops' own time  33.9 us (3%)
  between operations  23.7 us (2%)
    unnamed x19, waiting for transfers between devices  167 us
    unnamed x151, local copies, waits for them, and re-layouts  73.7 us
    psum x1, waiting for transfers between devices, body(): lax.psum(jnp.einsum('tf,df->td', pre_grad, proj_up, preferred_element_typ...  67.9 us
    psum x1, waiting for transfers between devices, body(): lax.psum(jnp.dot(cross_att, proj_cross_out, preferred_element_type=jnp.fl...  67 us
    psum x1, waiting for transfers between devices, body(): lax.psum(query_part.astype(jnp.bfloat16), 'tensor').astype(jnp.float32)  63.2 us
    psum x1, blocking collectives, body(): global_norm = jnp.sqrt(lax.psum(local_squares, ('dp', 'tensor')))  40.1 us
    all_gather x1, blocking collectives, body(): lax.all_gather(halves[0], 'dp', axis=1, tiled=True)  37.2 us
    dynamic_slice x36, local copies, waits for them, and re-layouts, body(): lax.map(self_forward, (self_rows[0], self_rows[1], self_rows[2], tgt_seg,...  36.5 us
  transfers between devices with their start and end apart: 14, of which 8 were waited for; matrix products, arithmetic and copies ran while one was open for 22% of the time, Pallas kernels for 0%

commit v1 on v0

v1 whole, which is shorter than its diff:
```python
from functools import partial
import math

import jax
import jax.numpy as jnp
from jax import lax
from jax.experimental import pallas as pl
from jax.experimental.pallas import tpu as pltpu
from jax.sharding import Mesh, PartitionSpec as P

HD = 64
EPS_NORM = 1e-05
NEG_FILL = -1000000000.0
BETA_ONE = 0.9
BETA_TWO = 0.999
EPS_ADAM = 1e-08
RATE_MATRIX = 0.05
RATE_OUTPUT = 0.25
RATE_NORMS = 0.75
DECAY_RATE = 0.1
CLIP_LIMIT = 1.0
GELU_COEF = 0.044715

BF = jnp.bfloat16
F32 = jnp.float32
RB = 256
PW = 768
MESH_ID = pl.DeviceIdType.MESH
VMEM_LIMIT = 60 * 1024 * 1024


def nn(a, b):
    return lax.dot_general(a, b, (((1,), (0,)), ((), ())), preferred_element_type=F32)


def nt(a, b):
    return lax.dot_general(a, b, (((1,), (1,)), ((), ())), preferred_element_type=F32)


def vm(n=1):
    return [pl.BlockSpec(memory_space=pltpu.VMEM)] * n


def anym(n=1):
    return [pl.BlockSpec(memory_space=pl.ANY)] * n


def sds(shape, dtype):
    return jax.ShapeDtypeStruct(shape, dtype)


def params(**kw):
    return pltpu.CompilerParams(vmem_limit_bytes=VMEM_LIMIT, **kw)


def block(i, size=RB):
    return pl.ds(pl.multiple_of(i * size, size), size)


def gelu_with_slope(values):
    root = math.sqrt(2.0 / math.pi)
    square = values * values
    tangent = jnp.tanh(values * (root + (root * GELU_COEF) * square))
    half = 0.5 + 0.5 * tangent
    output = values * half
    slope = half + 0.5 * output * (1.0 - tangent) * (2.0 * root + (6.0 * root * GELU_COEF) * square)
    return output, slope


def norm_stats(values):
    centre = values - jnp.mean(values, -1, keepdims=True)
    inverse = lax.rsqrt(jnp.mean(centre * centre, -1, keepdims=True) + EPS_NORM)
    return centre * inverse, inverse


def norm_forward(values, gain, shift):
    scaled, _ = norm_stats(values)
    return (scaled * gain + shift).astype(BF)


def norm_backward(upstream, values, gain):
    scaled, inverse = norm_stats(values)
    weighted = upstream * gain
    product = upstream * scaled
    result = inverse * (
        weighted
        - jnp.mean(weighted, -1, keepdims=True)
        - scaled * jnp.mean(weighted * scaled, -1, keepdims=True)
    )
    return result, jnp.sum(product, 0, keepdims=True), jnp.sum(upstream, 0, keepdims=True)


def fetch_row(src, dst, sem):
    rows = dst.shape[0]
    start = lax.axis_index("ta") * rows
    return pltpu.make_async_copy(src.at[pl.ds(start, rows)], dst, sem)


def join_groups(packed, joined):
    depth, width = packed.shape[1], packed.shape[2] // 4

    @pl.loop(0, depth // 128)
    def _(i):
        first, second = packed[0, block(i, 128), :], packed[1, block(i, 128), :]
        pieces = []
        for s in range(4):
            pieces += [first[:, s * width : (s + 1) * width], second[:, s * width : (s + 1) * width]]
        joined[block(i, 128), :] = jnp.concatenate(pieces, axis=1)


def split_groups(joined_rows, packed, rows):
    width = joined_rows.shape[1] // 8
    for t in range(2):
        packed[t, rows, :] = jnp.concatenate(
            [joined_rows[:, (2 * s + t) * width : (2 * s + t + 1) * width] for s in range(4)], axis=1
        ).astype(BF)


def transpose_into(src, dst):
    @pl.loop(0, src.shape[0] // RB)
    def _(i):
        dst[:, block(i)] = src[block(i), :].T


def head_masks(rows):
    lane = lax.broadcasted_iota(jnp.int32, (rows, 2 * HD), 1)
    return lane < HD


def keep_half(values, low_half, head):
    zero = jnp.zeros_like(values)
    return jnp.where(low_half, values, zero) if head == 0 else jnp.where(low_half, zero, values)


def attend(qkv, bias_of, causal, out, logsum, bias):
    rows, cols = out.shape
    pairs = cols // (2 * HD)

    def one(q_rows, keys, pair):
        lanes = block(pair, 2 * HD)
        k_lanes = pl.ds(pl.multiple_of(cols + pair * 2 * HD, 2 * HD), 2 * HD)
        v_lanes = pl.ds(pl.multiple_of(2 * cols + pair * 2 * HD, 2 * HD), 2 * HD)
        query, key, value = qkv[q_rows, lanes], qkv[0:keys, k_lanes], qkv[0:keys, v_lanes]
        low_half = head_masks(RB)
        outs, sums = [], []
        for head in range(2):
            scores = nt(keep_half(query, low_half, head), key) + bias[:, 0:keys]
            peak = jnp.max(scores, -1, keepdims=True)
            shifted = jnp.exp(scores - peak)
            total = jnp.sum(shifted, -1, keepdims=True)
            outs.append(nn(shifted.astype(BF), value) / total)
            sums.append(peak + jnp.log(total))
        out[q_rows, lanes] = jnp.where(low_half, outs[0], outs[1]).astype(BF)
        both = jnp.where(low_half, sums[0], sums[1]).T
        logsum[pair, :, q_rows] = jnp.concatenate([both[0:1], both[HD : HD + 1]], axis=0)

    if causal:
        for i in range(rows // RB):
            keys = (i + 1) * RB
            bias[:, 0:keys] = bias_of(i, keys)
            pl.loop(0, pairs)(partial(one, pl.ds(i * RB, RB), keys))
    else:

        @pl.loop(0, rows // RB)
        def _(i):
            bias[...] = bias_of(i, rows)
            pl.loop(0, pairs)(partial(one, block(i), rows))


def attend_back(qkv, attended, grad, logsum, bias_of, causal, dqkv, dk_sum, dv_sum, bias):
    rows, cols = attended.shape
    pairs = cols // (2 * HD)
    dk_sum[...] = jnp.zeros_like(dk_sum)
    dv_sum[...] = jnp.zeros_like(dv_sum)

    def one(q_rows, keys, pair):
        lanes = block(pair, 2 * HD)
        k_lanes = pl.ds(pl.multiple_of(cols + pair * 2 * HD, 2 * HD), 2 * HD)
        v_lanes = pl.ds(pl.multiple_of(2 * cols + pair * 2 * HD, 2 * HD), 2 * HD)
        query, key, value = qkv[q_rows, lanes], qkv[0:keys, k_lanes], qkv[0:keys, v_lanes]
        out_grad = grad[q_rows, lanes]
        low_half = head_masks(RB)
        low_keys = head_masks(keys)
        product = (out_grad.astype(F32) * attended[q_rows, lanes].astype(F32)).T
        dq = dk = dv = None
        for head in range(2):
            inner = jnp.sum(product[head * HD : (head + 1) * HD], 0, keepdims=True)
            q_head = keep_half(query, low_half, head)
            g_head = keep_half(out_grad, low_half, head)
            scores = nt(key, q_head) + bias[0:keys, :]
            weights = jnp.exp(scores - logsum[pair, head : head + 1, q_rows])
            weight_grad = nt(value, g_head)
            score_grad = (weights * (weight_grad - inner)).astype(BF)
            dv_part = nn(weights.astype(BF), g_head)
            dk_part = nn(score_grad, q_head)
            dq_part = nn(score_grad.T, keep_half(key, low_keys, head))
            dv = dv_part if dv is None else dv + dv_part
            dk = dk_part if dk is None else dk + dk_part
            dq = dq_part if dq is None else dq + dq_part
        dqkv[q_rows, lanes] = (dq * (1.0 / math.sqrt(HD))).astype(BF)
        dk_sum[0:keys, lanes] += dk
        dv_sum[0:keys, lanes] += dv

    if causal:
        for i in range(rows // RB):
            keys = (i + 1) * RB
            bias[0:keys, :] = bias_of(i, keys)
            pl.loop(0, pairs)(partial(one, pl.ds(i * RB, RB), keys))
    else:

        @pl.loop(0, rows // RB)
        def _(i):
            bias[...] = bias_of(i, rows)
            pl.loop(0, pairs)(partial(one, block(i), rows))

    @pl.loop(0, rows // RB)
    def _(i):
        dqkv[block(i), cols : 2 * cols] = dk_sum[block(i), :].astype(BF)
        dqkv[block(i), 2 * cols : 3 * cols] = dv_sum[block(i), :].astype(BF)


def self_bias(q_ids, k_ids, i, keys):
    same = q_ids[block(i), :] == k_ids[:, 0:keys]
    if not isinstance(i, int):
        raise ValueError("static block")
    q_pos = i * RB + lax.broadcasted_iota(jnp.int32, (RB, keys), 0)
    k_pos = lax.broadcasted_iota(jnp.int32, (RB, keys), 1)
    allowed = (same & (k_pos < q_pos)) | (k_pos == q_pos)
    return jnp.where(allowed, 0.0, NEG_FILL)


def self_bias_turned(q_ids, k_ids, i, keys):
    same = k_ids[0:keys, :] == q_ids[:, i * RB : (i + 1) * RB]
    q_pos = i * RB + lax.broadcasted_iota(jnp.int32, (keys, RB), 1)
    k_pos = lax.broadcasted_iota(jnp.int32, (keys, RB), 0)
    allowed = (same & (k_pos < q_pos)) | (k_pos == q_pos)
    return jnp.where(allowed, 0.0, NEG_FILL)


def cross_bias(q_ids, k_ids, i, keys):
    return jnp.where(q_ids[block(i), :] == k_ids[:, 0:keys], 0.0, NEG_FILL)


def cross_bias_turned(q_ids, k_ids, i, keys):
    return jnp.where(k_ids[0:keys, :] == q_ids[:, block(i)], 0.0, NEG_FILL)


def self_forward_kernel(
    target, packed, norms, q_ids, k_ids, part, qkv, normed, out, logsum, row, weights, bias, sem
):
    fetch = fetch_row(target, row, sem)
    fetch.start()
    join_groups(packed, weights)
    fetch.wait()
    cols = out.shape[1]

    @pl.loop(0, row.shape[0] // RB)
    def _(i):
        n = norm_forward(row[block(i), :].astype(F32), norms[0:1, :], norms[3:4, :])
        normed[block(i), :] = n
        projected = nn(n, weights[:, 0 : 3 * cols])
        qkv[block(i), 0:cols] = (projected[:, 0:cols].astype(BF).astype(F32) * (1.0 / math.sqrt(HD))).astype(BF)
        qkv[block(i), cols : 3 * cols] = projected[:, cols : 3 * cols].astype(BF)

    attend(qkv, partial(self_bias, q_ids, k_ids), True, out, logsum, bias)

    @pl.loop(0, row.shape[0] // RB)
    def _(i):
        part[block(i), :] = nt(out[block(i), :], weights[:, 3 * cols : 4 * cols]).astype(BF)


def cross_forward_kernel(
    target, own, other, memory, packed, norms, q_ids, k_ids,
    hidden, part, qkv, normed, out, logsum,
    row, mem_row, weights, bias, sem,
):
    fetch, fetch_mem = fetch_row(target, row, sem.at[0]), fetch_row(memory, mem_row, sem.at[1])
    fetch.start()
    fetch_mem.start()
    join_groups(packed, weights)
    fetch.wait()
    fetch_mem.wait()
    cols = out.shape[1]

    @pl.loop(0, row.shape[0] // RB)
    def _(i):
        h = row[block(i), :].astype(F32) + (own[block(i), :].astype(F32) + other[block(i), :].astype(F32))
        hidden[block(i), :] = h
        n = norm_forward(h, norms[1:2, :], norms[4:5, :])
        normed[block(i), :] = n
        q = nn(n, weights[:, 0:cols]).astype(BF).astype(F32) * (1.0 / math.sqrt(HD))
        qkv[block(i), 0:cols] = q.astype(BF)
        qkv[block(i), cols : 3 * cols] = nn(mem_row[block(i), :], weights[:, cols : 3 * cols]).astype(BF)

    attend(qkv, partial(cross_bias, q_ids, k_ids), False, out, logsum, bias)

    @pl.loop(0, row.shape[0] // RB)
    def _(i):
        part[block(i), :] = nt(out[block(i), :], weights[:, 3 * cols : 4 * cols]).astype(BF)


def feed_forward_kernel(
    hidden, own, other, cotangent, up, down, norms,
    hidden_two, part, grad_part, grad_up, grad_down,
    cot, normed, active, pre_grad, turned, sem,
):
    fetch = fetch_row(cotangent, cot, sem)
    fetch.start()
    fetch.wait()

    @pl.loop(0, hidden.shape[0] // RB)
    def _(i):
        h = hidden[block(i), :] + (own[block(i), :].astype(F32) + other[block(i), :].astype(F32))
        hidden_two[block(i), :] = h
        n = norm_forward(h, norms[2:3, :], norms[5:6, :])
        normed[block(i), :] = n
        e = cot[block(i), :]
        total = grad_total = None
        for t in range(2):
            activated, slope = gelu_with_slope(nn(n, up[t]))
            activated = activated.astype(BF)
            du = (nn(e, down[t]) * slope).astype(BF)
            active[t, block(i), :] = activated
            pre_grad[t, block(i), :] = du
            one, two = nt(activated, down[t]), nt(du, up[t])
            total = one if total is None else total + one
            grad_total = two if grad_total is None else grad_total + two
        part[block(i), :] = total.astype(BF)
        grad_part[block(i), :] = grad_total.astype(BF)

    for src, rhs, dst in ((normed, pre_grad, grad_up), (cot, active, grad_down)):
        transpose_into(src, turned)

        @pl.loop(0, turned.shape[0] // RB)
        def _(i):
            for t in range(2):
                dst[t, block(i), :] = nn(turned[block(i), :], rhs[t]).astype(BF)


def back_in(upstream_a, upstream_b, values, gain, residual, sums, rows):
    upstream = upstream_a[rows, :].astype(F32) + upstream_b[rows, :].astype(F32)
    delta, gain_part, shift_part = norm_backward(upstream, values, gain)
    sums[0:1, :] += gain_part
    sums[1:2, :] += shift_part
    return residual + delta


def cross_backward_kernel(
    hidden, own, other, cotangent, attended, qkv, logsum, normed, memory, packed, norms, q_ids, k_ids,
    residual, grads, part, mem_part, norm_sums,
    cot, mem_row, weights, low, grad, dqkv, dk_sum, dv_sum, bias, turned, joined, sem,
):
    fetch, fetch_mem = fetch_row(cotangent, cot, sem.at[0]), fetch_row(memory, mem_row, sem.at[1])
    fetch.start()
    fetch_mem.start()
    join_groups(packed, weights)
    norm_sums[...] = jnp.zeros_like(norm_sums)
    fetch.wait()
    fetch_mem.wait()
    cols = attended.shape[1]
    blocks = hidden.shape[0] // RB

    @pl.loop(0, blocks)
    def _(i):
        e = back_in(
            own, other, hidden[block(i), :], norms[2:3, :], cot[block(i), :].astype(F32), norm_sums, block(i)
        )
        residual[block(i), :] = e
        low[block(i), :] = e.astype(BF)
        grad[block(i), :] = nn(e.astype(BF), weights[:, 3 * cols : 4 * cols]).astype(BF)

    attend_back(
        qkv, attended, grad, logsum, partial(cross_bias_turned, q_ids, k_ids), False, dqkv, dk_sum, dv_sum, bias
    )

    @pl.loop(0, blocks)
    def _(i):
        part[block(i), :] = nt(dqkv[block(i), 0:cols], weights[:, 0:cols]).astype(BF)
        mem_part[block(i), :] = nt(dqkv[block(i), cols : 3 * cols], weights[:, cols : 3 * cols]).astype(BF)

    for src, rhs, first, last in ((normed, dqkv, 0, 1), (mem_row, dqkv, 1, 3), (low, attended, 3, 4)):
        transpose_into(src, turned)
        rhs_cols = slice(0, cols) if rhs is attended else slice(first * cols, last * cols)

        @pl.loop(0, turned.shape[0] // RB)
        def _(i):
            joined[block(i), first * cols : last * cols] = nn(turned[block(i), :], rhs[:, rhs_cols])

    @pl.loop(0, turned.shape[0] // RB)
    def _(i):
        split_groups(joined[block(i), :], grads, block(i))


def self_backward_kernel(
    hidden, own, other, residual, attended, qkv, logsum, normed, packed, norms, q_ids, k_ids,
    residual_out, grads, part, norm_sums,
    weights, low, grad, dqkv, dk_sum, dv_sum, bias, turned, joined,
):
    join_groups(packed, weights)
    norm_sums[...] = jnp.zeros_like(norm_sums)
    cols = attended.shape[1]
    blocks = hidden.shape[0] // RB

    @pl.loop(0, blocks)
    def _(i):
        e = back_in(own, other, hidden[block(i), :], norms[1:2, :], residual[block(i), :], norm_sums, block(i))
        residual_out[block(i), :] = e
        low[block(i), :] = e.astype(BF)
        grad[block(i), :] = nn(e.astype(BF), weights[:, 3 * cols : 4 * cols]).astype(BF)

    attend_back(
        qkv, attended, grad, logsum, partial(self_bias_turned, q_ids, k_ids), True, dqkv, dk_sum, dv_sum, bias
    )

    @pl.loop(0, blocks)
    def _(i):
        part[block(i), :] = nt(dqkv[block(i), :], weights[:, 0 : 3 * cols]).astype(BF)

    for src, rhs, first, last in ((normed, dqkv, 0, 3), (low, attended, 3, 4)):
        transpose_into(src, turned)

        @pl.loop(0, turned.shape[0] // RB)
        def _(i):
            joined[block(i), first * cols : last * cols] = nn(turned[block(i), :], rhs[...])

    @pl.loop(0, turned.shape[0] // RB)
    def _(i):
        split_groups(joined[block(i), :], grads, block(i))


def last_norm_kernel(target, own, other, residual, norms, grad_row, norm_sums, row, sem):
    fetch = fetch_row(target, row, sem)
    fetch.start()
    norm_sums[...] = jnp.zeros_like(norm_sums)
    fetch.wait()

    @pl.loop(0, row.shape[0] // RB)
    def _(i):
        grad_row[block(i), :] = back_in(
            own, other, row[block(i), :].astype(F32), norms[0:1, :], residual[block(i), :], norm_sums, block(i)
        )


def places():
    dp, ta = lax.axis_index("dp"), lax.axis_index("ta")
    return lax.div(dp, 2), lax.rem(dp, 2), ta


class Peers:
    def __init__(self, nz):
        self.nz = nz
        self.z, self.x, self.ta = places()
        self.ox, self.ot = 1 - self.x, 1 - self.ta
        self.x_peer = {"dp": self.z * 2 + self.ox}
        self.y_peer = {"ta": self.ot}
        self.core_peer = {"tb": 1 - lax.axis_index("tb")}

    def up(self, j):
        return lax.rem(self.z + j, self.nz)

    def down(self, j):
        return lax.rem(self.z + (self.nz - j), self.nz)

    def z_peer(self, j):
        return {"dp": self.up(j) * 2 + self.x}

    def greet(self, core=False):
        barrier = pltpu.get_barrier_semaphore()
        others = [self.z_peer(j) for j in range(1, self.nz)] + [self.x_peer, self.y_peer]
        others += [self.core_peer] if core else []
        for other in others:
            pl.semaphore_signal(barrier, inc=1, device_id=other, device_id_type=MESH_ID)
        pl.semaphore_wait(barrier, len(others))


def gather_copies(nz):
    return (nz - 1) + 2 * nz + nz


class Gather:
    def __init__(self, peers, out, send, recv):
        self.p, self.out, self.send, self.recv = peers, out, send, recv
        nz = peers.nz
        self.half = nz // 2
        self.first_x, self.first_y, self.first_d = nz - 1, 2 * nz - 1, 3 * nz - 1

    def copy(self, t, d, index, peer):
        slot = self.out.at[t, d]
        return pltpu.make_async_remote_copy(
            src_ref=slot, dst_ref=slot, send_sem=self.send.at[index], recv_sem=self.recv.at[index],
            device_id=peer, device_id_type=MESH_ID,
        )

    def mine(self, j, turn_x=False, turn_t=False):
        p = self.p
        return (p.ot if turn_t else p.ta), p.down(j) * 2 + (p.ox if turn_x else p.x)

    def start(self):
        p = self.p
        t, d = self.mine(0)
        for j in range(1, p.nz):
            self.copy(t, d, j - 1, p.z_peer(j)).start()
        self.plane(0)

    def plane(self, j):
        t, d = self.mine(j)
        self.copy(t, d, self.first_x + j, self.p.x_peer).start()
        self.copy(t, d, self.first_y + j, self.p.y_peer).start()

    def after_z(self, j):
        t, d = self.mine(j)
        self.copy(t, d, j - 1, self.p.x_peer).wait_recv()
        self.plane(j)

    def after_plane(self, j):
        t, d = self.mine(j, turn_x=True)
        self.copy(t, d, self.first_x + j, self.p.x_peer).wait_recv()
        if j < self.half:
            self.copy(t, d, self.first_d + j, self.p.y_peer).start()
        t, d = self.mine(j, turn_t=True)
        self.copy(t, d, self.first_y + j, self.p.y_peer).wait_recv()
        if j >= self.half:
            self.copy(t, d, self.first_d + j, self.p.x_peer).start()

    def finish(self):
        p = self.p
        for j in range(p.nz):
            t, d = self.mine(j, turn_x=True, turn_t=True)
            self.copy(t, d, self.first_d + j, p.x_peer).wait_recv()
        for index in range(gather_copies(p.nz)):
            t, d = self.mine(0)
            self.copy(t, d, index, p.x_peer).wait_send()


def gather_kernel(nz, count, *refs):
    shards, outs, sems = refs[:count], refs[count : 2 * count], refs[2 * count :]
    peers = Peers(nz)
    peers.greet()
    works = []
    for k in range(count):
        out = outs[k]
        out[peers.ta, peers.z * 2 + peers.x] = shards[k][...]
        works.append(Gather(peers, out, sems[0].at[k], sems[1].at[k]))
        works[k].start()
    for k in range(count):
        for j in range(1, nz):
            works[k].after_z(j)
    for k in range(count):
        for j in range(nz):
            works[k].after_plane(j)
    for k in range(count):
        works[k].finish()


def gather_all(shards, dp_size):
    nz = dp_size // 2
    count = len(shards)
    copies = gather_copies(nz)
    return pl.pallas_call(
        partial(gather_kernel, nz, count),
        name="gather_weights",
        out_shape=[sds((2, dp_size) + s.shape, s.dtype) for s in shards],
        in_specs=vm(count),
        out_specs=vm(count),
        scratch_shapes=[pltpu.SemaphoreType.DMA((count, copies)), pltpu.SemaphoreType.DMA((count, copies))],
        compiler_params=params(collective_id=0, has_side_effects=True),
    )(*shards)


class Reduce:
    def __init__(self, peers, part, landing, relay, send, recv):
        self.p, self.part, self.landing, self.relay, self.send, self.recv = peers, part, landing, relay, send, recv
        nz = peers.nz
        self.half = nz // 2
        self.first_x, self.first_y, self.first_z = nz, 2 * nz, 3 * nz

    def slot(self, j, turn_x=False, turn_t=False):
        p = self.p
        return self.part.at[(p.ot if turn_t else p.ta), p.up(j) * 2 + (p.ox if turn_x else p.x)]

    def copy(self, src, index, peer):
        return pltpu.make_async_remote_copy(
            src_ref=src, dst_ref=self.landing.at[index], send_sem=self.send.at[index], recv_sem=self.recv.at[index],
            device_id=peer, device_id_type=MESH_ID,
        )

    def arrived(self, index):
        self.copy(self.slot(0), index, self.p.x_peer).wait_recv()
        return self.landing[index].astype(F32)

    def start(self):
        p = self.p
        for j in range(p.nz):
            diagonal = self.slot(j, turn_x=True, turn_t=True)
            self.copy(diagonal, j, p.x_peer if j < self.half else p.y_peer).start()
        for j in range(p.nz):
            if j < self.half:
                self.copy(self.slot(j, turn_x=True), self.first_x + j, p.x_peer).start()
            else:
                self.copy(self.slot(j, turn_t=True), self.first_y + j, p.y_peer).start()

    def pass_on(self, j):
        p = self.p
        kwargs = {"turn_t": True} if j < self.half else {"turn_x": True}
        slot = self.relay.at[j]
        slot[...] = (self.slot(j, **kwargs)[...].astype(F32) + self.arrived(j)).astype(slot.dtype)
        if j < self.half:
            self.copy(slot, self.first_y + j, p.y_peer).start()
        else:
            self.copy(slot, self.first_x + j, p.x_peer).start()

    def along_z(self, j):
        total = self.slot(j)[...].astype(F32) + self.arrived(self.first_x + j) + self.arrived(self.first_y + j)
        if j == 0:
            return total
        slot = self.relay.at[self.p.nz + j - 1]
        slot[...] = total.astype(slot.dtype)
        self.copy(slot, self.first_z + j - 1, self.p.z_peer(j)).start()
        return None

    def finish(self, total):
        for j in range(1, self.p.nz):
            total = total + self.arrived(self.first_z + j - 1)
        for index in range(gather_copies(self.p.nz)):
            self.copy(self.slot(0), index, self.p.x_peer).wait_send()
        return total


def reduce_kernel(nz, count, tensor_size, norm_index, *refs):
    parts, outs, norm_out = refs[:count], refs[count : 2 * count], refs[2 * count]
    rest = refs[2 * count + 1 :]
    landings, relays = rest[:count], rest[count : 2 * count]
    stage, heard, send, recv, sends, recvs = rest[2 * count :]
    peers = Peers(nz)
    peers.greet(core=True)
    works = [Reduce(peers, parts[k], landings[k], relays[k], send.at[k], recv.at[k]) for k in range(count)]
    for w in works:
        w.start()
    for w in works:
        for j in range(nz):
            w.pass_on(j)
    for w in works:
        for j in range(1, nz):
            w.along_z(j)
    squares = jnp.zeros((1, 1), F32)
    for k, w in enumerate(works):
        total = w.finish(w.along_z(0))
        outs[k][...] = total
        share = jnp.sum(jnp.sum(total * total, -1, keepdims=True), 0, keepdims=True)
        squares = squares + (share / tensor_size if k == norm_index else share)

    def swap(step, peer, value):
        stage[step] = value
        copy = pltpu.make_async_remote_copy(
            src_ref=stage.at[step], dst_ref=heard.at[step], send_sem=sends.at[step], recv_sem=recvs.at[step],
            device_id=peer, device_id_type=MESH_ID,
        )
        copy.start()
        copy.wait()
        return value + heard[step]

    value = jnp.broadcast_to(squares, (8, 128))
    for step, peer in enumerate((peers.core_peer, peers.x_peer, peers.y_peer)):
        value = swap(step, peer, value)
    heard[3 + peers.z] = value
    copies = []
    for j in range(1, nz):
        copies.append(
            pltpu.make_async_remote_copy(
                src_ref=heard.at[3 + peers.z], dst_ref=heard.at[3 + peers.z], send_sem=sends.at[2 + j],
                recv_sem=recvs.at[2 + j], device_id=peers.z_peer(j), device_id_type=MESH_ID,
            )
        )
        copies[-1].start()
    for j in range(1, nz):
        pltpu.make_async_remote_copy(
            src_ref=heard.at[3 + peers.z], dst_ref=heard.at[3 + peers.down(j)], send_sem=sends.at[2 + j],
            recv_sem=recvs.at[2 + j], device_id=peers.z_peer(j), device_id_type=MESH_ID,
        ).wait_recv()
    for copy in copies:
        copy.wait_send()
    total = heard[3]
    for k in range(1, nz):
        total = total + heard[3 + k]
    norm_out[...] = total


def reduce_all(parts, dp_size, tensor_size, norm_index):
    nz = dp_size // 2
    count = len(parts)
    copies = gather_copies(nz)
    shard = [p.shape[2:] for p in parts]
    return pl.pallas_call(
        partial(reduce_kernel, nz, count, tensor_size, norm_index),
        name="reduce_gradients",
        out_shape=[sds(s, F32) for s in shard] + [sds((8, 128), F32)],
        in_specs=vm(count),
        out_specs=vm(count + 1),
        scratch_shapes=[pltpu.VMEM((copies,) + s, BF) for s in shard]
        + [pltpu.VMEM((2 * nz - 1,) + s, BF) for s in shard]
        + [
            pltpu.VMEM((3, 8, 128), F32),
            pltpu.VMEM((3 + nz, 8, 128), F32),
            pltpu.SemaphoreType.DMA((count, copies)),
            pltpu.SemaphoreType.DMA((count, copies)),
            pltpu.SemaphoreType.DMA((2 + nz,)),
            pltpu.SemaphoreType.DMA((2 + nz,)),
        ],
        compiler_params=params(collective_id=1, has_side_effects=True),
    )(*parts)


def adam_update(weight, gradient, first, second, clip_factor, bias_one, bias_two, rate, decay):
    scaled = gradient * clip_factor
    first_new = BETA_ONE * first + (1.0 - BETA_ONE) * scaled
    second_new = BETA_TWO * second + (1.0 - BETA_TWO) * scaled * scaled
    first_hat = first_new / bias_one
    second_hat = second_new / bias_two
    weight_new = weight - rate * (first_hat / (jnp.sqrt(second_hat) + EPS_ADAM) + decay * weight)
    return weight_new, weight_new.astype(BF), first_new, second_new


RATES = (
    (RATE_MATRIX, DECAY_RATE),
    (RATE_OUTPUT, DECAY_RATE),
    (RATE_MATRIX, DECAY_RATE),
    (RATE_OUTPUT, DECAY_RATE),
    (RATE_MATRIX, DECAY_RATE),
    (RATE_MATRIX, DECAY_RATE),
    (RATE_NORMS, 0.0),
)


def shard_gradients(reduced, width):
    g_self, g_cross, g_up, g_down, g_norms = reduced
    cut = [
        [g[:, s * width : (s + 1) * width] for s in range(4)] for g in (g_self, g_cross)
    ]
    return (cut[0][:3], cut[0][3].T, cut[1][:3], cut[1][3].T, g_up, g_down.T, g_norms)


def adam_kernel(*refs):
    reduced, squares, biases = refs[:5], refs[5], refs[6]
    state, norm_out, outs = refs[7:28], refs[28], refs[29:]
    width = state[3].shape[0]
    norm = jnp.sqrt(squares[...])
    norm_out[...] = norm
    clip = (CLIP_LIMIT / jnp.maximum(norm, CLIP_LIMIT))[0:1, 0:1]
    values = [r[...] for r in reduced]
    shape = state[18].shape
    values[4] = values[4][0 : shape[0], 0 : shape[1]]
    gradients = shard_gradients(values, width)
    for k, (rate, decay) in enumerate(RATES):
        weight, first, second = state[3 * k : 3 * k + 3]
        into = outs[4 * k : 4 * k + 4]
        if isinstance(gradients[k], list):
            for s in range(3):
                new = adam_update(
                    weight[s], gradients[k][s], first[s], second[s], clip, biases[0], biases[1], rate, decay
                )
                for ref, value in zip(into, new):
                    ref[s] = value
        else:
            new = adam_update(
                weight[...], gradients[k], first[...], second[...], clip, biases[0], biases[1], rate, decay
            )
            for ref, value in zip(into, new):
                ref[...] = value


def swap_core(value):
    return lax.ppermute(value, "tb", [(0, 1), (1, 0)])


def both_rows(row, ta, tb):
    half = row.shape[0] // 2
    mine = lax.dynamic_slice_in_dim(row, tb * half, half).astype(BF)
    got = lax.ppermute(mine, "ta", [(0, 1), (1, 0)])
    rest = swap_core(got)
    other = jnp.where(tb == 0, jnp.concatenate([got, rest]), jnp.concatenate([rest, got])).astype(F32)
    return jnp.where(ta == 0, jnp.concatenate([row, other]), jnp.concatenate([other, row]))


def body(target, memory, cotangent, tgt_seg, mem_seg, pad_len, step_count, *state):
    dp_size, tensor_size = lax.axis_size("dp"), lax.axis_size("ta") * lax.axis_size("tb")
    ta, tb = lax.axis_index("ta"), lax.axis_index("tb")
    self_in, self_out, cross_in, cross_out, ffn_in, ffn_out, norm_params = state[::3]
    length, depth = tgt_seg.shape[1], target.shape[1]
    mem_length = mem_seg.shape[1]
    width, span = self_out.shape
    cols = 2 * width
    own_transfers = span % 16 == 0

    def pack(w_in, w_out):
        return jnp.concatenate([w_in[0], w_in[1], w_in[2], w_out.T], axis=1).astype(BF)

    norm_shard = jnp.zeros((16, 128), BF).at[: norm_params.shape[0], :span].set(norm_params.astype(BF))
    shards = [pack(self_in, self_out), pack(cross_in, cross_out), ffn_in.astype(BF), ffn_out.T.astype(BF), norm_shard]
    if own_transfers:
        gathered = gather_all(shards, dp_size)
    else:
        gathered = [lax.all_gather(lax.all_gather(s, "dp", axis=0), "ta", axis=0) for s in shards]
    w_self, w_cross, w_up, w_down = [g.reshape(2, depth, g.shape[3]) for g in gathered[:4]]
    norms = gathered[4][0][:, :, :span].transpose(1, 0, 2).reshape(16, depth).astype(F32)

    tgt_ids = lax.dynamic_slice_in_dim(tgt_seg, ta, 1)
    mem_ids = lax.dynamic_slice_in_dim(mem_seg, ta, 1)
    pad = lax.dynamic_slice_in_dim(pad_len, ta, 1)
    key_ids = jnp.where(jnp.arange(length)[None, :] < length - pad[:, None], tgt_ids, -1)
    tgt_col, mem_col, key_col = tgt_ids.reshape(length, 1), mem_ids.reshape(mem_length, 1), key_ids.reshape(length, 1)

    row_bf, row_f32 = sds((length, depth), BF), sds((length, depth), F32)
    mem_bf = sds((mem_length, depth), BF)
    qkv_bf, att_bf = sds((length, 3 * cols), BF), sds((length, cols), BF)
    logsum = sds((cols // 128, 2, length), F32)
    grads = sds((2, depth, 4 * width), BF)
    sums = sds((8, depth), F32)
    v_row, v_att = pltpu.VMEM((length, depth), BF), pltpu.VMEM((length, cols), BF)
    v_mem = pltpu.VMEM((mem_length, depth), BF)
    v_joined = pltpu.VMEM((depth, 4 * cols), BF)
    v_sum = pltpu.VMEM((mem_length, cols), F32)

    def flops(macs, nbytes):
        return pl.CostEstimate(flops=2 * macs, bytes_accessed=nbytes, transcendentals=0)

    dense = length * depth

    def call(kernel, name, ins, outs, scratch, macs):
        arrays = [a for a, _ in ins]
        return pl.pallas_call(
            kernel,
            name=name,
            out_shape=outs,
            in_specs=[vm()[0] if spec else anym()[0] for _, spec in ins],
            out_specs=vm(len(outs)),
            scratch_shapes=scratch,
            compiler_params=params(),
            cost_estimate=flops(macs, 20 << 20),
        )(*arrays)

    part_one, qkv_one, normed_one, att_one, lse_one = call(
        self_forward_kernel,
        "self_forward",
        [(target, 0), (w_self, 1), (norms, 1), (tgt_col, 1), (key_ids, 1)],
        [row_bf, qkv_bf, row_bf, att_bf, logsum],
        [v_row, v_joined, pltpu.VMEM((RB, length), F32), pltpu.SemaphoreType.DMA],
        dense * 4 * cols * 2,
    )
    hidden_one, part_two, qkv_two, normed_two, att_two, lse_two = call(
        cross_forward_kernel,
        "cross_forward",
        [(target, 0), (part_one, 1), (swap_core(part_one), 1), (memory, 0), (w_cross, 1), (norms, 1)]
        + [(tgt_col, 1), (mem_ids, 1)],
        [row_f32, row_bf, qkv_bf, row_bf, att_bf, logsum],
        [v_row, v_mem, v_joined, pltpu.VMEM((RB, mem_length), F32), pltpu.SemaphoreType.DMA((2,))],
        dense * 4 * cols * 2,
    )
    hidden = w_up.shape[2]
    v_hidden = pltpu.VMEM((2, length, hidden), BF)
    hidden_two, part_three, grad_three, g_up, g_down = call(
        feed_forward_kernel,
        "feed_forward",
        [(hidden_one, 1), (part_two, 1), (swap_core(part_two), 1), (cotangent, 0), (w_up, 1), (w_down, 1), (norms, 1)],
        [row_f32, row_bf, row_bf, sds((2, depth, hidden), BF), sds((2, depth, hidden), BF)],
        [v_row, v_row, v_hidden, v_hidden, pltpu.VMEM((depth, length), BF), pltpu.SemaphoreType.DMA],
        dense * hidden * 12,
    )
    block_out = hidden_two + (part_three.astype(F32) + swap_core(part_three).astype(F32))
    residual_two, g_cross, grad_two, mem_part, sums_three = call(
        cross_backward_kernel,
        "cross_backward",
        [(hidden_two, 1), (grad_three, 1), (swap_core(grad_three), 1), (cotangent, 0), (att_two, 1), (qkv_two, 1)]
        + [(lse_two, 1), (normed_two, 1), (memory, 0), (w_cross, 1), (norms, 1), (tgt_ids, 1), (mem_col, 1)],
        [row_f32, grads, row_bf, mem_bf, sums],
        [v_row, v_mem, v_joined, v_row, v_att, pltpu.VMEM((length, 3 * cols), BF), v_sum, v_sum]
        + [pltpu.VMEM((mem_length, RB), F32), pltpu.VMEM((depth, length), BF), pltpu.VMEM((depth, 4 * cols), F32)]
        + [pltpu.SemaphoreType.DMA((2,))],
        dense * 4 * cols * 4,
    )
    grad_memory = mem_part.astype(F32) + swap_core(mem_part).astype(F32)
    residual_one, g_self, grad_one, sums_two = call(
        self_backward_kernel,
        "self_backward",
        [(hidden_one, 1), (grad_two, 1), (swap_core(grad_two), 1), (residual_two, 1), (att_one, 1), (qkv_one, 1)]
        + [(lse_one, 1), (normed_one, 1), (w_self, 1), (norms, 1), (tgt_ids, 1), (key_col, 1)],
        [row_f32, grads, row_bf, sums],
        [v_joined, v_row, v_att, pltpu.VMEM((length, 3 * cols), BF), v_sum, v_sum]
        + [pltpu.VMEM((length, RB), F32), pltpu.VMEM((depth, length), BF), pltpu.VMEM((depth, 4 * cols), F32)],
        dense * 4 * cols * 4,
    )
    grad_target, sums_one = call(
        last_norm_kernel,
        "last_norm",
        [(target, 0), (grad_one, 1), (swap_core(grad_one), 1), (residual_one, 1), (norms, 1)],
        [row_f32, sums],
        [v_row, pltpu.SemaphoreType.DMA],
        dense,
    )

    all_sums = jnp.stack([sums_one[0], sums_two[0], sums_three[0], sums_one[1], sums_two[1], sums_three[1]])
    norm_parts = all_sums.reshape(6, dp_size, span).transpose(1, 0, 2)
    norm_parts = jnp.zeros((dp_size, 16, 128), BF).at[:, :6, :span].set(norm_parts.astype(BF))
    norm_parts = jnp.broadcast_to(norm_parts[None], (2,) + norm_parts.shape)
    parts = [g.reshape(2, dp_size, span, g.shape[2]) for g in (g_self, g_cross, g_up, g_down)] + [norm_parts]
    step_float = step_count.astype(F32)
    biases = jnp.stack([1.0 - jnp.power(BETA_ONE, step_float), 1.0 - jnp.power(BETA_TWO, step_float)])
    if own_transfers:
        *reduced, squares = reduce_all(parts, dp_size, tensor_size, 4)
        updated = pl.pallas_call(
            adam_kernel,
            name="adam",
            out_shape=[sds((8, 128), F32)]
            + [sds(w.shape, dt) for w in state[::3] for dt in (F32, BF, F32, F32)],
            in_specs=vm(6) + [pl.BlockSpec(memory_space=pltpu.SMEM)] + vm(21),
            out_specs=vm(29),
            compiler_params=params(),
        )(*reduced, squares, biases, *state)
        global_norm, updated = updated[0][0, 0], updated[1:]
    else:
        reduced = [
            lax.psum_scatter(lax.psum_scatter(p.astype(F32), "ta", scatter_dimension=0), "dp", scatter_dimension=0)
            for p in parts
        ]
        reduced[4] = reduced[4][:6, :span]
        total = sum(jnp.sum(r * r) for r in reduced[:4]) + jnp.sum(reduced[4] * reduced[4]) / tensor_size
        global_norm = jnp.sqrt(lax.psum(total, ("dp", "ta", "tb")))
        clip = CLIP_LIMIT / jnp.maximum(global_norm, CLIP_LIMIT)
        updated = []
        for k, g in enumerate(shard_gradients(reduced, width)):
            g = jnp.stack(g) if isinstance(g, list) else g
            weight, first, second = state[3 * k : 3 * k + 3]
            updated += adam_update(weight, g, first, second, clip, biases[0], biases[1], *RATES[k])
    return (
        global_norm,
        both_rows(block_out, ta, tb),
        both_rows(grad_target, ta, tb),
        both_rows(grad_memory, ta, tb),
        *updated,
    )


def solution(mesh):
    dp_size, tensor_size = mesh.shape["dp"], mesh.shape["tensor"]
    grid = Mesh(mesh.devices.reshape(dp_size, 2, tensor_size // 2), ("dp", "ta", "tb"))
    tensor = ("ta", "tb")
    rows = P("dp", None)
    place = (
        P(None, "dp", tensor),
        P(tensor, "dp"),
        P(None, "dp", tensor),
        P(tensor, "dp"),
        P("dp", tensor),
        P(tensor, "dp"),
        P(None, "dp"),
    )
    return jax.shard_map(
        body,
        mesh=grid,
        in_specs=(rows,) * 5 + (P("dp"), P()) + tuple(p for p in place for _ in range(3)),
        out_specs=(P(), rows, rows, rows) + tuple(p for p in place for _ in range(4)),
        check_vma=False,
    )
```

time: 1310 us -> 522 us (0.40)
  Pallas kernels: 0 us -> 404 us
  waiting for transfers between devices: 387 us -> 38.7 us
  local copies, waits for them, and re-layouts: 319 us -> 30.4 us
  blocking collectives: 205 us -> 0 us
  matrix products: 183 us -> 0 us
  other arithmetic: 150 us -> 28.6 us
  loops' own time: 33.9 us -> 0 us
  between operations: 23.7 us -> 2.6 us
    pallas_call x0 -> x9, Pallas kernels: none -> 404 us  [the longest x6 168 us: call(): pl.pallas_call(kernel, name=name, out_shape=outs, in_specs=[vm()[0] if sp...]
    psum x5 -> x0, waiting for transfers between devices: 219 us -> none  [the longest x1 67.9 us: body(): lax.psum(jnp.einsum('tf,df->td', pre_grad, proj_up, preferred_element_typ...]
    dot_general x74 -> x0, matrix products: 171 us -> none  [the longest x8 20.1 us: one_block(): jnp.einsum('qhd,khd->hqk', grad_block, value_heads, preferred_element_typ...]
    unnamed x19 -> x0, waiting for transfers between devices: 167 us -> none
    all_gather x5 -> x0, blocking collectives: 165 us -> none  [the longest x1 37.2 us: body(): lax.all_gather(halves[0], 'dp', axis=1, tiled=True)]
    reduce_sum x24 -> x0, other arithmetic: 57.9 us -> none  [the longest x8 14.4 us: one_block(): totals = jnp.sum(shifted, -1, keepdims=True)]
    dynamic_slice x68 -> x2, local copies, waits for them, and re-layouts: 59 us -> 1.19 us  [the longest x1 0.6 us: body(): mem_ids = lax.dynamic_slice_in_dim(mem_seg, ta, 1)]
    unnamed x151 -> x47, local copies, waits for them, and re-layouts: 73.7 us -> 19.3 us
  transfers between devices with their start and end apart: 14 -> 13, of which waited for: 8 -> 6; matrix products, arithmetic and copies ran while one was open for 22% -> 7% of each run, Pallas kernels for 0% -> 36%
where the time goes in v1:
time: 522 us; the launch traced here: 512 us
  Pallas kernels  404 us (77%)
  waiting for transfers between devices  38.7 us (7%)
  local copies, waits for them, and re-layouts  30.4 us (6%)
  other arithmetic  28.6 us (5%)
  starting transfers between devices  7.36 us (1%)
    pallas_call x6, Pallas kernels, call(): pl.pallas_call(kernel, name=name, out_shape=outs, in_specs=[vm()[0] if sp...  168 us
    pallas_call x1, Pallas kernels, reduce_all(): pl.pallas_call(partial(reduce_kernel, nz, count, tensor_size, norm_index)...  134 us
    pallas_call x1, Pallas kernels, gather_all(): pl.pallas_call(partial(gather_kernel, nz, count), name='gather_weights',...  96.4 us
    ppermute x3, waiting for transfers between devices, both_rows(): got = lax.ppermute(mine, 'ta', [(0, 1), (1, 0)])  27 us
    unnamed x47, local copies, waits for them, and re-layouts  19.3 us
    ppermute x10, waiting for transfers between devices, swap_core(): return lax.ppermute(value, 'tb', [(0, 1), (1, 0)])  11.7 us
  transfers between devices with their start and end apart: 13, of which 6 were waited for; matrix products, arithmetic and copies ran while one was open for 7% of the time, Pallas kernels for 36%

profile of v1, /device:TPU:0, one launch (start us, length us, event | category | flops | bytes accessed | tf_op | source)
XLA Modules:
  0.0 511.9 jit_solution(10014224706545184653)
XLA Ops:
  0.7 1.0 copy.71
  1.7 1.0 convert.50
  2.7 1.0 copy.72
  3.7 1.0 convert.52
  4.7 1.6 convert_element_type.60.refs_2_
  6.4 1.6 convert_bitcast_fusion.refs_3_
  10.1 96.4 %gather_weights.1 = (bf16[2,8,96,768]{3,2,1,0:T(8,128)(2,1)}, bf16[2,8,96,768]{3,2,1,0:T(8,128)(2,1)}, bf16[2,8,96,768]{3,2,1,0:T(8,128)(2,1)}, bf16[2,8,96,768]{3,2,1,0:T(8,128)(2,1)}, bf16[2,8,16,128]{3,2,1,0:T(8,128)(2,1)}) custom-call(bf16[96,768]{1,0:T(8,128)(2,1)} %get-tuple-element.268.refs_0_, bf16[96,768]{1,0:T(8,128)(2,1)} %get-tuple-element.269.refs_1_, ...), custom_call_target="tpu_custom_call" | custom-call | tf_op jit(solution)/shard_map/gather_weights/pallas_call | solution.py:559
  109.9 1.0 copy.74.q_ids
  110.9 22.2 %self_forward.1 = (bf16[1024,768]{1,0:T(8,128)(2,1)}, bf16[1024,1152]{1,0:T(8,128)(2,1)}, bf16[1024,768]{1,0:T(8,128)(2,1)}, bf16[1024,384]{1,0:T(8,128)(2,1)}, f32[3,2,1024]{2,1,0:T(2,128)}) custom-call(bf16[2048,768]{1,0:T(8,128)(2,1)} %target.5, bf16[2,768,768]{2,1,0:T(8,128)(2,1)} %bitcast.56, f32[16,768]{1,0:T(8,128)} %reshape.195.norms, ...), custom_call_target="tpu_custom_call" | custom-call | flops 4831838208 | bytes 20971520 | tf_op jit(solution)/shard_map/self_forward/pallas_call | solution.py:830
  133.9 3.0 collective-permute-done.other
  136.9 1.1 copy-done.16
  138.0 27.8 %cross_forward.1 = (f32[1024,768]{1,0:T(8,128)}, bf16[1024,768]{1,0:T(8,128)(2,1)}, bf16[1024,1152]{1,0:T(8,128)(2,1)}, bf16[1024,768]{1,0:T(8,128)(2,1)}, bf16[...) custom-call(bf16[2048,768]{1,0:T(8,128)(2,1)} %target.5, bf16[1024,768]{1,0:T(8,128)(2,1)} %get-tuple-element.125.own, ...), custom_call_target="tpu_custom_call" | custom-call | flops 4831838208 | bytes 20971520 | tf_op jit(solution)/shard_map/cross_forward/pallas_call | solution.py:830
  166.0 3.5 collective-permute-done.1.other
  169.5 1.1 copy-done.17
  170.6 28.5 %feed_forward.1 = (f32[1024,768]{1,0:T(8,128)}, bf16[1024,768]{1,0:T(8,128)(2,1)}, bf16[1024,768]{1,0:T(8,128)(2,1)}, bf16[2,768,768]{2,1,0:T(8,128)(2,1)}, bf16[2,768,768]{2,1,0:T(8,128)(2,1)}) custom-call(f32[1024,768]{1,0:T(8,128)} %get-tuple-element.127.hidden, bf16[1024,768]{1,0:T(8,128)(2,1)} %get-tuple-element.128.own, bf16[1024,768]{1,0:T(8,128)(2,1)} %copy-done.17, ...), custom_call_target="tpu_custom_call" | custom-call | flops 14495514624 | bytes 20971520 | tf_op jit(solution)/shard_map/feed_forward/pallas_call | solution.py:830
  199.3 1.0 copy.76.k_ids
  200.4 2.4 collective-permute-done.2.other
  202.8 1.2 copy-done.15
  204.1 44.3 %cross_backward.1 = (f32[1024,768]{1,0:T(8,128)}, bf16[2,768,768]{2,1,0:T(8,128)(2,1)}, bf16[1024,768]{1,0:T(8,128)(2,1)}, bf16[1024,768]{1,0:T(8,128)(2,1)}, f32[8,768]{1,0:T(8,128)}) custom-call(f32[1024,768]{1,0:T(8,128)} %get-tuple-element.131.hidden, bf16[1024,768]{1,0:T(8,128)(2,1)} %get-tuple-element.132.own, bf16[1024,768]{1,0:T(8,128)(2,1)} %copy-done.15, ...), custom_call_target="tpu_custom_call" | custom-call | flops 9663676416 | bytes 20971520 | tf_op jit(solution)/shard_map/cross_backward/pallas_call | solution.py:830
  248.9 1.1 copy.77.k_ids
  250.1 2.7 collective-permute-done.3.other
  252.9 1.1 copy-done.14
  254.0 36.1 %self_backward.1 = (f32[1024,768]{1,0:T(8,128)}, bf16[2,768,768]{2,1,0:T(8,128)(2,1)}, bf16[1024,768]{1,0:T(8,128)(2,1)}, f32[8,768]{1,0:T(8,128)}) custom-call(f32[1024,768]{1,0:T(8,128)} %get-tuple-element.127.hidden, bf16[1024,768]{1,0:T(8,128)(2,1)} %get-tuple-element.137.own, bf16[1024,768]{1,0:T(8,128)(2,1)} %copy-done.14, ...), custom_call_target="tpu_custom_call" | custom-call | flops 9663676416 | bytes 20971520 | tf_op jit(solution)/shard_map/self_backward/pallas_call | solution.py:830
  290.4 2.6 add_add_fusion
  293.1 2.5 collective-permute-start.6
  295.6 1.8 convert_add_fusion
  297.5 1.0 dynamic-slice_convert_fusion
  298.5 1.0 collective-permute-start.11
  299.5 14.5 %collective-permute-done.6 = bf16[512,768]{1,0:T(8,128)(2,1)} collective-permute-done((bf16[512,768]{1,0:T(8,128)(2,1)S(1)}, bf16[512,768]{1,0:T(8,128)(2,1)}, u32[]{:S(2)}, u32[]{:S(2)}) %collective-permute-start.6) | collective-permute-done | bytes 786464 | tf_op jit(solution)/shard_map/ppermute | solution.py:778
  315.7 1.9 copy.80.refs_23_
  317.6 1.9 copy.81.refs_24_
  320.1 8.7 %last_norm.1 = (f32[1024,768]{1,0:T(8,128)}, f32[8,768]{1,0:T(8,128)}) custom-call(bf16[2048,768]{1,0:T(8,128)(2,1)} %target.5, bf16[1024,768]{1,0:T(8,128)(2,1)} %get-tuple-element.147.own, bf16[1024,768]{1,0:T(8,128)(2,1)} %collective-permute-done.4.other, f32[1024,768]{1,0:T(8,128)} %get-tuple-element.148.residual, f32[16,768]{1,0:T(8,128)} %reshape.195.norms), custom_call_target="tpu_custom_call" | custom-call | flops 1572864 | bytes 20971520 | tf_op jit(solution)/shard_map/last_norm/pallas_call | solution.py:830
  328.8 1.6 dynamic-slice_convert_fusion.1
  330.5 2.1 collective-permute-start.8
  332.9 2.3 fusion
  335.2 3.1 maximum_select_fusion
  338.4 12.5 %collective-permute-done.8 = bf16[512,768]{1,0:T(8,128)(2,1)} collective-permute-done((bf16[512,768]{1,0:T(8,128)(2,1)S(1)}, bf16[512,768]{1,0:T(8,128)(2,1)}, u32[]{:S(2)}, u32[]{:S(2)}) %collective-permute-start.8) | collective-permute-done | bytes 786464 | tf_op jit(solution)/shard_map/ppermute | solution.py:778
  351.7 134.3 %reduce_gradients.1 = (f32[96,768]{1,0:T(8,128)}, f32[96,768]{1,0:T(8,128)}, f32[96,768]{1,0:T(8,128)}, f32[96,768]{1,0:T(8,128)}, f32[16,128]{1,0:T(8,128)}, /*index=5*/f32[8,128]{1,0:T(8,128)}) custom-call(bf16[2,8,96,768]{3,2,1,0:T(8,128)(2,1)} %bitcast.50, bf16[2,8,96,768]{3,2,1,0:T(8,128)(2,1)} %bitcast.49, bf16[2,8,96,768]{3,2,1,0:T(8,128)(2,1)} %bitcast.47, ...), custom_call_target="tpu_custom_call" | custom-call | tf_op jit(solution)/shard_map/reduce_gradients/pallas_call | solution.py:693
  486.0 5.9 %adam.1 = (f32[8,128]{1,0:T(8,128)}, f32[3,96,192]{2,1,0:T(8,128)}, bf16[3,96,192]{2,1,0:T(8,128)(2,1)}, f32[3,96,192]{2,1,0:T(8,128)}, f32[3,96,192]{2,1,0:T(8,...) custom-call(f32[96,768]{1,0:T(8,128)} %get-tuple-element.152.refs_0_, ...), custom_call_target="tpu_custom_call" | custom-call | tf_op jit(solution)/shard_map/adam/pallas_call | solution.py:909
  491.9 1.2 slice.116
  493.1 1.9 copy.82
  495.0 1.7 copy.83
  496.7 1.9 copy.84
  498.6 1.9 copy.85
  500.5 2.2 fusion.2
  502.6 3.1 maximum_select_fusion.2
  505.8 2.3 fusion.1
  508.6 3.1 maximum_select_fusion.1
  (78 shorter events, 10.2 us)
Async XLA Ops:
  0.7 132.6 %copy-start = (s32[2,1024]{1,0:T(2,128)S(1)}, s32[2,1024]{1,0:T(2,128)}, u32[]{:S(2)}) copy-start(s32[2,1024]{1,0:T(2,128)} %param.36) | copy-start | bytes 24580
  0.7 107.3 %copy-start.18 = (s32[2]{0:T(128)S(1)}, s32[2]{0:T(128)}, u32[]{:S(2)}) copy-start(s32[2]{0:T(128)} %param.37) | copy-start | bytes 28
  0.7 108.6 %copy-start.13 = (s32[2,1024]{1,0:T(2,128)S(1)}, s32[2,1024]{1,0:T(2,128)}, u32[]{:S(2)}) copy-start(s32[2,1024]{1,0:T(2,128)} %param.35) | copy-start | bytes 24580
  109.9 23.3 %copy-start.11 = (s32[1,1024]{1,0:T(1,128)}, s32[1,1024]{1,0:T(1,128)S(1)}, u32[]{:S(2)}) copy-start(s32[1,1024]{1,0:T(1,128)S(1)} %get-tuple-element.255.q_ids) | copy-start | bytes 12292
  133.2 3.7 collective-permute-start
  136.9 1.1 copy-start.16
  165.8 3.7 collective-permute-start.1
  169.5 1.1 copy-start.17
  199.1 3.7 collective-permute-start.2
  202.8 1.2 copy-start.15
  204.1 44.9 %copy-start.12 = (s32[1,1024]{1,0:T(1,128)S(1)}, s32[1,1024]{1,0:T(1,128)}, u32[]{:S(2)}) copy-start(s32[1,1024]{1,0:T(1,128)} %get-tuple-element.254.k_ids) | copy-start | bytes 12292
  248.3 4.5 collective-permute-start.3
  248.5 41.8 %collective-permute-start.5 = (bf16[1024,768]{1,0:T(8,128)(2,1)}, bf16[1024,768]{1,0:T(8,128)(2,1)}, u32[]{:S(2)}, u32[]{:S(2)}) collective-permute-start(bf16[1024,768]{1,0:T(8,128)(2,1)} %get-tuple-element.159), channel_id=1, source_target_pairs={{0,1},{1,0},{2,3},{3,2},{4,5},{5,4},{6,7},{7,6},{8,9},{9,8},{10,11... | collective-permute-start | bytes 4718600 | tf_op jit(solution)/shard_map/ppermute | solution.py:772
  250.0 45.6 %collective-permute-start.10 = (bf16[1024,768]{1,0:T(8,128)(2,1)}, bf16[1024,768]{1,0:T(8,128)(2,1)}, u32[]{:S(2)}, u32[]{:S(2)}) collective-permute-start(bf16[1024,768]{1,0:T(8,128)(2,1)} %get-tuple-element.161), channel_id=1, source_target_pairs={{0,1},{1,0},{2,3},{3,2},{4,5},{5,4},{6,7},{7,6},{8,9},{9,8},{10,11... | collective-permute-start | bytes 4718600 | tf_op jit(solution)/shard_map/ppermute | solution.py:772
  252.9 1.2 copy-start.14
  254.0 36.4 %copy-start.5 = (f32[1024,768]{1,0:T(8,128)S(1)}, f32[1024,768]{1,0:T(8,128)}, u32[]{:S(2)}) copy-start(f32[1024,768]{1,0:T(8,128)} %get-tuple-element.131.hidden) | copy-start | bytes 9437188
  290.2 5.5 %copy-start.6 = (bf16[1024,768]{1,0:T(8,128)(2,1)S(1)}, bf16[1024,768]{1,0:T(8,128)(2,1)}, u32[]{:S(2)}) copy-start(bf16[1024,768]{1,0:T(8,128)(2,1)} %get-tuple-element.161) | copy-start | bytes 4718596
  290.2 29.9 %collective-permute-start.4 = (bf16[1024,768]{1,0:T(8,128)(2,1)}, bf16[1024,768]{1,0:T(8,128)(2,1)}, u32[]{:S(2)}, u32[]{:S(2)}) collective-permute-start(bf16[1024,768]{1,0:T(8,128)(2,1)} %get-tuple-element.147.own), channel_id=1, source_target_pairs={{0,1},{1,0},{2,3},{3,2},{4,5},{5,4},{6,7},{7,6},{8,9},{9,8},{10,11... | collective-permute-start | bytes 4718600 | tf_op jit(solution)/shard_map/ppermute | solution.py:772
  293.0 4.5 copy-start.2
  293.1 20.9 %copy-start.7 = (f32[768,96]{0,1:T(8,128)S(1)}, f32[768,96]{0,1:T(8,128)}, u32[]{:S(2)}) copy-start(f32[768,96]{0,1:T(8,128)} %param.54) | copy-start | bytes 884740
  293.1 20.9 %collective-permute-start.6 = (bf16[512,768]{1,0:T(8,128)(2,1)S(1)}, bf16[512,768]{1,0:T(8,128)(2,1)}, u32[]{:S(2)}, u32[]{:S(2)}) collective-permute-start(bf16[512,768]{1,0:T(8,128)(2,1)S(1)} %dynamic-slice_convert_fusion.2), channel_id=1, source_target_pairs={{0,2},{2,0},{1,3},{3,1},{4,6},{6,4},{5,7},{7,5},{8,10},{10,8},{9,1... | collective-permute-start | bytes 2359304 | tf_op jit(solution)/shard_map/ppermute | solution.py:778
  297.5 22.6 %copy-start.8 = (f32[8,768]{1,0:T(8,128)S(1)}, f32[8,768]{1,0:T(8,128)}, u32[]{:S(2)}) copy-start(f32[8,768]{1,0:T(8,128)} %get-tuple-element.151) | copy-start | bytes 73732
  297.5 22.6 %copy-start.9 = (f32[8,768]{1,0:T(8,128)S(1)}, f32[8,768]{1,0:T(8,128)}, u32[]{:S(2)}) copy-start(f32[8,768]{1,0:T(8,128)} %get-tuple-element.150) | copy-start | bytes 73732
  298.5 34.1 %collective-permute-start.11 = (bf16[512,768]{1,0:T(8,128)(2,1)}, bf16[512,768]{1,0:T(8,128)(2,1)}, u32[]{:S(2)}, u32[]{:S(2)}) collective-permute-start(bf16[512,768]{1,0:T(8,128)(2,1)} %dynamic-slice_convert_fusion), channel_id=1, source_target_pairs={{0,2},{2,0},{1,3},{3,1},{4,6},{6,4},{5,7},{7,5},{8,10},{10,8},{9,1... | collective-permute-start | bytes 2359304 | tf_op jit(solution)/shard_map/ppermute | solution.py:778
  314.1 18.8 %collective-permute-start.7 = (bf16[512,768]{1,0:T(8,128)(2,1)}, bf16[512,768]{1,0:T(8,128)(2,1)}, u32[]{:S(2)}, u32[]{:S(2)}) collective-permute-start(bf16[512,768]{1,0:T(8,128)(2,1)} %collective-permute-done.6), channel_id=1, source_target_pairs={{0,1},{1,0},{2,3},{3,2},{4,5},{5,4},{6,7},{7,6},{8,9},{9,8},{10,11... | collective-permute-start | bytes 2359304 | tf_op jit(solution)/shard_map/ppermute | solution.py:772
  328.8 6.4 %copy-start.3 = (f32[1024,768]{1,0:T(8,128)S(1)}, f32[1024,768]{1,0:T(8,128)}, u32[]{:S(2)}) copy-start(f32[1024,768]{1,0:T(8,128)} %copy-done.2) | copy-start | bytes 9437188
  330.5 20.4 %collective-permute-start.8 = (bf16[512,768]{1,0:T(8,128)(2,1)S(1)}, bf16[512,768]{1,0:T(8,128)(2,1)}, u32[]{:S(2)}, u32[]{:S(2)}) collective-permute-start(bf16[512,768]{1,0:T(8,128)(2,1)S(1)} %dynamic-slice_convert_fusion.1), channel_id=1, source_target_pairs={{0,2},{2,0},{1,3},{3,1},{4,6},{6,4},{5,7},{7,5},{8,10},{10,8},{9,1... | collective-permute-start | bytes 2359304 | tf_op jit(solution)/shard_map/ppermute | solution.py:778
  332.6 167.9 %collective-permute-start.12 = (bf16[512,768]{1,0:T(8,128)(2,1)}, bf16[512,768]{1,0:T(8,128)(2,1)}, u32[]{:S(2)}, u32[]{:S(2)}) collective-permute-start(bf16[512,768]{1,0:T(8,128)(2,1)} %collective-permute-done.11), channel_id=1, source_target_pairs={{0,1},{1,0},{2,3},{3,2},{4,5},{5,4},{6,7},{7,6},{8,9},{9,8},{10,11... | collective-permute-start | bytes 2359304 | tf_op jit(solution)/shard_map/ppermute | solution.py:772
  335.2 3.2 copy-start.10
  350.9 154.9 %collective-permute-start.9 = (bf16[512,768]{1,0:T(8,128)(2,1)}, bf16[512,768]{1,0:T(8,128)(2,1)}, u32[]{:S(2)}, u32[]{:S(2)}) collective-permute-start(bf16[512,768]{1,0:T(8,128)(2,1)} %collective-permute-done.8), channel_id=1, source_target_pairs={{0,1},{1,0},{2,3},{3,2},{4,5},{5,4},{6,7},{7,6},{8,9},{9,8},{10,11... | collective-permute-start | bytes 2359304 | tf_op jit(solution)/shard_map/ppermute | solution.py:772
  505.8 2.8 copy-start.4
  508.6 3.1 copy-start.1
